TPU v7x, 128 devices: a whole 4x4x4 slice. The times are simulated.
128 devices in a mesh: dp: 16 (over z, y), tensor: 4 (over x), layer: 2 (over core).
Axes of the slice: x: 4, y: 4, z: 4, core: 2. Of those that a mesh axis runs over, the one named last changes fastest.
Arguments:
- hidden: bfloat16 [2, 16, 1024, 9216], P('layer', 'dp', None, 'tensor')
- out_grad: bfloat16 [2, 16, 1024, 2304], P('layer', 'dp', None, 'tensor'), may hold values from -6 to 6
- lengths: int32 [16], P('dp'), may hold values from 64 to 1024, as said below
- noise: float32 [2, 2304, 9216], P('layer', 'dp', 'tensor'), may hold values from -6 to 6
Outputs:
- noised_grad: bfloat16 [2, 2304, 9216], P('layer', None, 'tensor')
Inputs may be any that keep to these rules, and one draw needn't show every extreme that they name: `lengths`: the first sequence is full and the second has 64 tokens.
All inputs are finite; a program needn't handle non-finite values.
Results may differ from a plain program's by a relative error of at most 0.019.
Values may be sent and summed in bfloat16 or wider, within the bound.
A program may use at most 192 MiB of HBM per device.

v0:
```python
import jax
import jax.numpy as jnp
from jax import lax
from jax.sharding import PartitionSpec as P


def on_device(hidden, out_grad, lengths, noise):
    seq_len = hidden.shape[2]
    positions = lax.broadcasted_iota(jnp.int32, (lengths.shape[0], seq_len), 1)
    valid = positions < lengths[:, None]
    kept = jnp.where(valid[None, :, :, None], hidden, jnp.zeros((), hidden.dtype))[0]
    grads_full = lax.all_gather(out_grad, "tensor", axis=3, tiled=True)[0]
    width = grads_full.shape[2]
    units = kept.shape[2] * lax.axis_size("tensor")
    layers = lax.axis_size("layer")
    bound = jnp.sqrt(jnp.float32(seq_len * layers * units * width / 64.0))
    seqs_total = lengths.shape[0] * lax.axis_size("dp")
    gram_hidden = jnp.einsum("stf,suf->stu", kept, kept, preferred_element_type=jnp.float32)
    gram_grads = jnp.einsum(
        "stk,suk->stu", grads_full, grads_full, preferred_element_type=jnp.float32
    )
    partial_sq = jnp.sum(gram_hidden * gram_grads, axis=(1, 2))
    squares = lax.psum(partial_sq, ("tensor", "layer"))
    factor = jnp.minimum(jnp.float32(1.0), bound / jnp.sqrt(squares + 1e-06))
    share = lax.psum_scatter(
        jnp.einsum(
            "s,skf->kf",
            factor,
            jnp.einsum("stk,stf->skf", grads_full, kept, preferred_element_type=jnp.float32),
        ).astype(jnp.bfloat16),
        "dp",
        scatter_dimension=0,
        tiled=True,
    ).astype(jnp.float32)
    noised = ((share + noise[0]) / seqs_total).astype(jnp.bfloat16)
    whole = lax.all_gather(noised, "dp", axis=0, tiled=True)
    return whole[None]


def solution(mesh):
    placed = (
        P("layer", "dp", None, "tensor"),
        P("layer", "dp", None, "tensor"),
        P("dp"),
        P("layer", "dp", "tensor"),
    )
    return jax.shard_map(
        on_device, mesh=mesh, in_specs=placed, out_specs=P("layer", None, "tensor"), check_vma=False
    )
```

profile of v0, /device:TPU:0, one launch (start us, length us, event | category | flops | bytes accessed | tf_op | source)
XLA Modules:
  0.0 320.7 jit_solution(11148134368332904575)
XLA Ops:
  6.5 0.0 all-gather.3.cloned.1.call-start
  6.5 0.7 all-gather.3.cloned.1.call-update
  7.3 0.0 reduce-scatter.4.cloned.1.call-start
  8.0 56.1 %all-gather.3.cloned.1.call-done = bf16[1,1,1024,2304]{2,3,1,0:T(8,128)(2,1)} async-done(((bf16[1,1,1024,576]{2,3,1,0:T(8,128)(2,1)}), bf16[1,1,1024,2304]{2,3,1,0:T(8,128)(2,1)}) %all-gather.3.cloned.1.call-update) | async-done | bytes 4718608 | tf_op jit(solution)/shard_map/all_gather | solution.py:12
  64.1 8.3 %fusion.3 = f32[1024,1024]{1,0:T(8,128)S(1)} fusion(bf16[1,1,1024,2304]{2,3,1,0:T(8,128)(2,1)} %all-gather.3.cloned.1.call-done), kind=kOutput, calls=%fused_computation.4 | convolution fusion | flops 4831838208 | bytes 8912896 | tf_op jit(solution)/shard_map/stk,suk->stu/dot_general | solution.py:19
  72.5 9.9 %multiply_reduce_fusion = f32[]{:T(128)} fusion(f32[1024,1024]{1,0:T(8,128)S(1)} %fusion.3, bf16[1,1,1024,2304]{3,2,1,0:T(8,128)(2,1)} %param.4, pred[1024]{0:T(1024)(128)(4,1)S(1)} %iota_compare_fusion), kind=kOutput, calls=%fused_computation.10 | convolution fusion | flops 4836294656 | bytes 8913924 | tf_op jit(solution)/shard_map/stf,suf->stu/dot_general | solution.py:18
  82.4 13.5 %psum.7 = f32[1]{0:T(128)} all-reduce(f32[1]{0:T(128)} %bitcast.3), channel_id=1, replica_groups=mesh['dp'=16,'tensor'=4,'layer'=2] {'tensor','layer'}, use_global_device_ids=true, to_apply=%region_1.2 | all-reduce | flops 1 | bytes 8 | tf_op jit(solution)/shard_map/psum | solution.py:23
  96.6 17.6 %fusion.1 = bf16[2304,2304]{0,1:T(8,128)(2,1)} fusion(f32[]{:T(128)} %bitcast.4, bf16[1,1,1024,2304]{2,3,1,0:T(8,128)(2,1)} %all-gather.3.cloned.1.call-done, bf16[1,1,1024,2304]{3,2,1,0:T(8,128)(2,1)} %param.4, pred[1024]{0:T(1024)(128)(4,1)S(1)} %iota_compare_fusion), kind=kOutput, calls=%fused_computation.2 | convolution fusion | flops 10884612096 | bytes 20055044 | tf_op jit(solution)/shard_map/stk,stf->skf/dot_general | solution.py:29
  114.2 14.9 %copy.9 = bf16[2304,2304]{1,0:T(8,128)(2,1)} copy(bf16[2304,2304]{0,1:T(8,128)(2,1)} %fusion.1) | data formatting | bytes 21233664
  129.2 0.0 reduce-scatter.4.cloned.1.call-update
  129.2 0.0 all-gather.5.cloned.1.call-start
  129.2 1.9 copy.7
  131.1 87.7 %reduce-scatter.4.cloned.1.call-done = bf16[144,2304]{1,0:T(8,128)(2,1)} async-done(((bf16[2304,2304]{1,0:T(8,128)(2,1)}), bf16[144,2304]{1,0:T(8,128)(2,1)}) %reduce-scatter.4.cloned.1.call-update) | async-done | bytes 663568
  218.8 1.5 copy.10
  220.3 1.3 fusion.9
  221.6 2.3 copy.8
  223.9 0.0 all-gather.5.cloned.1.call-update
  223.9 80.5 %all-gather.5.cloned.1.call-done = bf16[2304,2304]{1,0:T(8,128)(2,1)} async-done(((bf16[144,2304]{1,0:T(8,128)(2,1)}), bf16[2304,2304]{1,0:T(8,128)(2,1)}) %all-gather.5.cloned.1.call-update) | async-done | bytes 10616848 | tf_op jit(solution)/shard_map/all_gather | solution.py:36
  304.4 9.8 %copy.13 = bf16[1,2304,2304]{2,1,0:T(8,128)(2,1)} copy(bf16[1,2304,2304]{2,1,0:T(8,128)(2,1)} %bitcast.26) | data formatting | bytes 21233664
  (1 shorter events, 0.0 us)
Async XLA Ops:
  6.5 57.6 %all-gather.3.cloned.1.call-start = ((), (), s32[]{:S(2)}) async-start(), calls=%async_computation.1 | async-start | bytes 5898240 | tf_op jit(solution)/shard_map/all_gather | solution.py:12
  7.3 211.6 %reduce-scatter.4.cloned.1.call-start = ((), (), s32[]{:S(2)}) async-start(), calls=%async_computation.3 | async-start | bytes 11280384
  129.2 175.2 %all-gather.5.cloned.1.call-start = ((), (), s32[]{:S(2)}) async-start(), calls=%async_computation.2 | async-start | bytes 11280384 | tf_op jit(solution)/shard_map/all_gather | solution.py:36
Sparse Core Ops, SparseCore 0:
  9.0 55.0 all-gather.2
  129.3 89.4 reduce-scatter.3
  224.0 80.2 all-gather.4
where the time goes:
time: 322 us; the launch traced here: 321 us
  waiting for transfers between devices  225 us (70%)
  matrix products  35.9 us (11%)
  local copies, waits for them, and re-layouts  30.3 us (9%)
  between operations  14.5 us (5%)
  blocking collectives  13.5 us (4%)
    unnamed x4, waiting for transfers between devices  88.5 us
    all_gather x1, waiting for transfers between devices, on_device(): whole = lax.all_gather(noised, 'dp', axis=0, tiled=True)  80.5 us
    all_gather x1, waiting for transfers between devices, on_device(): grads_full = lax.all_gather(out_grad, 'tensor', axis=3, tiled=True)[0]  56.1 us
    unnamed x4, local copies, waits for them, and re-layouts  28.1 us
    dot_general x1, matrix products, on_device(): jnp.einsum('stk,stf->skf', grads_full, kept, preferred_element_type=jnp.f...  17.6 us
    psum x1, blocking collectives, on_device(): squares = lax.psum(partial_sq, ('tensor', 'layer'))  13.5 us
    dot_general x1, matrix products, on_device(): jnp.einsum('stf,suf->stu', kept, kept, preferred_element_type=jnp.float32)  9.93 us
    dot_general x1, matrix products, on_device(): jnp.einsum('stk,suk->stu', grads_full, grads_full, preferred_element_type...  8.35 us
  transfers between devices with their start and end apart: 3, of which 3 were waited for; matrix products, arithmetic and copies ran while one was open for 1% of the time, Pallas kernels for 0%

commit v1 on v0

v1 whole, which is shorter than its diff:
```python
import functools

import jax
import jax.numpy as jnp
from jax import lax
from jax.experimental import pallas as pl
from jax.experimental.pallas import tpu as pltpu
from jax.sharding import PartitionSpec as P

MESH = pl.DeviceIdType.MESH
RING = 4
F32 = jnp.float32
BF16 = jnp.bfloat16


def kernel(bound, ot_hbm, h_hbm, noise_hbm, out_hbm,
           h_v, ot_v, g, r1, r2, fw, p1, p2, pf, nz, fin, sq, nrm, fac,
           load_sem, x_send, x_recv, raw_send, r1_recv, r2_recv, fw_send, fw_recv,
           p_send, p1_recv, p2_recv, pf_recv, nz_send, nz_recv, nrm_send, nrm_recv,
           fac_send, fac_recv, ag1_send, ag1_recv, ag2_send, ag2_recv, own_sem):
    dp = lax.axis_index("dp")
    x = lax.axis_index("tensor")
    core = lax.axis_index("layer")
    z, y = dp // RING, dp % RING
    block, tokens = ot_hbm.shape
    units = h_hbm.shape[1]
    piece = block // RING
    half = units // 2
    up = (piece // 32) * 16 + 16 * (piece // 16 % 2)
    down = piece - up

    def turn(i, by):
        return (i + by + RING) % RING

    z_up, z_down = {"dp": turn(z, 1) * RING + y}, {"dp": turn(z, -1) * RING + y}
    y_up, y_down = {"dp": z * RING + turn(y, 1)}, {"dp": z * RING + turn(y, -1)}
    x_up, x_down = {"tensor": turn(x, 1)}, {"tensor": turn(x, -1)}
    swap = {"dp": y * RING + z}
    q, r = (z, y), (y, z)
    q_up, q_down = (z_up, y_up), (z_down, y_down)
    r_up, r_down = (y_up, z_up), (y_down, z_down)
    cols = (pl.ds(0, half), pl.ds(half, half))

    def rows(b, p, start=0, size=None):
        return pl.ds(pl.multiple_of(b * block + p * piece + start, 16), piece if size is None else size)

    def remote(src, dst, send, recv, device):
        pltpu.make_async_remote_copy(src_ref=src, dst_ref=dst, send_sem=send, recv_sem=recv,
                                     device_id=device, device_id_type=MESH).start()

    def await_bytes(ref, sem):
        pltpu.make_async_copy(ref, ref, sem).wait()

    me = x * 2 + core
    group = []
    for k in range(1, 2 * RING):
        other = (me + k) % (2 * RING)
        group.append({"tensor": other // 2, "layer": other % 2})

    load_h = pltpu.make_async_copy(h_hbm, h_v, load_sem.at[0])
    load_h.start()
    load_o = pltpu.make_async_copy(ot_hbm, ot_v.at[pl.ds(pl.multiple_of(x * block, 16), block)], load_sem.at[1])
    load_o.start()
    load_n = pltpu.make_async_copy(noise_hbm.at[:, cols[1]], nz.at[1], load_sem.at[2])
    load_n.start()

    barrier = pltpu.get_barrier_semaphore()
    for device in group + [z_up, z_down, y_up, y_down]:
        pl.semaphore_signal(barrier, inc=1, device_id=device, device_id_type=MESH)

    @pl.when(z != y)
    def _():
        pl.semaphore_signal(barrier, inc=1, device_id=swap, device_id_type=MESH)
        pl.semaphore_wait(barrier, 12)

    @pl.when(z == y)
    def _():
        pl.semaphore_wait(barrier, 11)

    load_o.wait()

    def x_start(m):
        own = m < RING
        b, p = jnp.where(own, x, turn(x, -1)), jnp.where(own, m, m - 4)
        at = ot_v.at[rows(b, p)]
        remote(at, at, x_send.at[0, m], x_recv.at[0, m], x_up)
        b, p = jnp.where(own, x, turn(x, 1)), jnp.where(own, m, m - 2)
        at = ot_v.at[rows(b, p)]
        remote(at, at, x_send.at[1, m], x_recv.at[1, m], x_down)

    x_start(jnp.int32(0))
    x_start(jnp.int32(1))

    @pl.when(z != y)
    def _():
        remote(noise_hbm.at[:, cols[0]], nz.at[0], nz_send, nz_recv, swap)

    @pl.when(z == y)
    def _():
        pltpu.make_async_copy(noise_hbm.at[:, cols[0]], nz.at[0], nz_recv).start()

    sq[...] = jnp.zeros_like(sq)
    load_h.wait()

    def product(ba, pa, bb, pb):
        wide = sq.shape[1]

        @pl.loop(0, units // wide)
        def _(n):
            at = pl.ds(pl.multiple_of(n * wide, wide), wide)
            left = jnp.concatenate([ot_v[rows(ba, pa)], ot_v[rows(bb, pb)]], axis=0)
            out = jnp.dot(left, h_v[:, at], preferred_element_type=F32)
            sq[...] += jnp.sum((out * out).reshape(2 * piece // 8, 8, wide), axis=0)
            low = out.astype(BF16)
            g[rows(ba, pa), at] = low[:piece]
            g[rows(bb, pb), at] = low[piece:]

    def send_raw(b, p):
        for h in range(2):
            away = turn(p - q[h], 0)
            upper = g.at[rows(b, p, 0, up), cols[h]]
            lower = g.at[rows(b, p, up, down), cols[h]]

            @pl.when(away == 1)
            def _():
                remote(lower, r2.at[h, b, pl.ds(up, down)], raw_send.at[h, b], r2_recv.at[h, b], q_up[h])

            @pl.when(away == 2)
            def _():
                remote(upper, r1.at[h, b, pl.ds(0, up)], raw_send.at[h, b], r1_recv.at[h, b], q_up[h])
                remote(lower, r1.at[h, b, pl.ds(up, down)], raw_send.at[h, b], r1_recv.at[h, b], q_down[h])

            @pl.when(away == 3)
            def _():
                remote(upper, r2.at[h, b, pl.ds(0, up)], raw_send.at[h, b], r2_recv.at[h, b], q_down[h])

    @pl.loop(0, 2)
    def _(i):
        product(x, 2 * i, x, 2 * i + 1)
        send_raw(x, 2 * i)
        send_raw(x, 2 * i + 1)

    @pl.loop(0, 6)
    def _(i):
        near = i < RING
        ba, pa = jnp.where(near, turn(x, -1), turn(x, 2)), jnp.where(near, i, i - 4)
        bb, pb = jnp.where(near, turn(x, 1), turn(x, 2)), jnp.where(near, i, i - 2)
        await_bytes(ot_v.at[rows(ba, pa)], x_recv.at[0, i])
        await_bytes(ot_v.at[rows(bb, pb)], x_recv.at[1, i])

        @pl.when(i < 4)
        def _():
            await_bytes(ot_v.at[pl.ds(0, piece)], x_send.at[0, i])
            await_bytes(ot_v.at[pl.ds(0, piece)], x_send.at[1, i])
            x_start(i + 2)

        product(ba, pa, bb, pb)
        send_raw(ba, pa)
        send_raw(bb, pb)

    nrm[pl.ds(me, 1)] = (sq[:, :128] + sq[:, 128:])[None]
    for device in group:
        remote(nrm.at[me], nrm.at[me], nrm_send, nrm_recv, device)
    await_bytes(nrm.at[pl.ds(0, 7)], nrm_recv)
    total = jnp.sum(jnp.sum(nrm[...], axis=0), keepdims=True)
    factor = jnp.minimum(jnp.float32(1.0), bound / jnp.sqrt(total + 1e-06))
    fac[0] = jnp.broadcast_to(factor, fac.shape[1:])
    for slot, device in ((1, z_up), (2, z_down), (3, y_up), (4, y_down)):
        remote(fac.at[0], fac.at[slot], fac_send, fac_recv, device)
    await_bytes(fac.at[pl.ds(1, 4)], fac_recv)
    scale = fac[0, 0:1, 0:1]
    before = (fac[1, 0:1, 0:1], fac[3, 0:1, 0:1])
    after = (fac[2, 0:1, 0:1], fac[4, 0:1, 0:1])

    def strips(size, body):
        @pl.loop(0, size // 16)
        def _(n):
            body(pl.multiple_of(n * 16, 16))

    def away_of(i):
        return jnp.where(i == 0, 2, jnp.where(i == 1, 1, jnp.where(i == 2, 3, 0)))

    @pl.loop(0, RING)
    def _(i):
        for h in range(2):
            b = turn(r[h], away_of(i))
            await_bytes(r1.at[h, b], r1_recv.at[h, b])

            def upper(n):
                at = rows(b, turn(q[h], 1), n, 16)
                g[at, cols[h]] = (scale * g[at, cols[h]].astype(F32)
                                  + before[h] * r1[h, b, pl.ds(n, 16)].astype(F32)).astype(BF16)

            strips(up, upper)
            remote(g.at[rows(b, turn(q[h], 1), 0, up), cols[h]], fw.at[h, b, pl.ds(0, up)],
                   fw_send.at[h, b], fw_recv.at[h, b], q_up[h])

            def lower(n):
                at = rows(b, turn(q[h], -1), up + n, 16)
                g[at, cols[h]] = (scale * g[at, cols[h]].astype(F32)
                                  + after[h] * r1[h, b, pl.ds(up + n, 16)].astype(F32)).astype(BF16)

            strips(down, lower)
            remote(g.at[rows(b, turn(q[h], -1), up, down), cols[h]], fw.at[h, b, pl.ds(up, down)],
                   fw_send.at[h, b], fw_recv.at[h, b], q_down[h])

    @pl.loop(0, RING)
    def _(i):
        away = away_of(i)
        for h in range(2):
            b = turn(r[h], away)
            await_bytes(r2.at[h, b], r2_recv.at[h, b])
            await_bytes(fw.at[h, b], fw_recv.at[h, b])

            def gathered(other):
                def body(n):
                    at = rows(b, q[h], n, 16)
                    g[at, cols[h]] = (scale * g[at, cols[h]].astype(F32)
                                      + fw[h, b, pl.ds(n, 16)].astype(F32)
                                      + other * r2[h, b, pl.ds(n, 16)].astype(F32)).astype(BF16)
                return body

            strips(up, gathered(after[h]))
            strips(down, lambda n: gathered(before[h])(up + n))
            upper = g.at[rows(b, q[h], 0, up), cols[h]]
            lower = g.at[rows(b, q[h], up, down), cols[h]]

            @pl.when(away == 1)
            def _():
                remote(lower, p2.at[h, pl.ds(up, down)], p_send.at[h], p2_recv.at[h], r_up[h])

            @pl.when(away == 2)
            def _():
                remote(upper, p1.at[h, pl.ds(0, up)], p_send.at[h], p1_recv.at[h], r_up[h])
                remote(lower, p1.at[h, pl.ds(up, down)], p_send.at[h], p1_recv.at[h], r_down[h])

            @pl.when(away == 3)
            def _():
                remote(upper, p2.at[h, pl.ds(0, up)], p_send.at[h], p2_recv.at[h], r_down[h])

    for h in range(2):
        await_bytes(p1.at[h], p1_recv.at[h])

        def upper(n):
            at = rows(turn(r[h], 1), q[h], n, 16)
            g[at, cols[h]] = (g[at, cols[h]].astype(F32) + p1[h, pl.ds(n, 16)].astype(F32)).astype(BF16)

        strips(up, upper)
        remote(g.at[rows(turn(r[h], 1), q[h], 0, up), cols[h]], pf.at[h, pl.ds(0, up)],
               p_send.at[h], pf_recv.at[h], r_up[h])

        def lower(n):
            at = rows(turn(r[h], -1), q[h], up + n, 16)
            g[at, cols[h]] = (g[at, cols[h]].astype(F32) + p1[h, pl.ds(up + n, 16)].astype(F32)).astype(BF16)

        strips(down, lower)
        remote(g.at[rows(turn(r[h], -1), q[h], up, down), cols[h]], pf.at[h, pl.ds(up, down)],
               p_send.at[h], pf_recv.at[h], r_down[h])

    load_n.wait()
    await_bytes(nz.at[0], nz_recv)
    for h in range(2):
        await_bytes(p2.at[h], p2_recv.at[h])
        await_bytes(pf.at[h], pf_recv.at[h])

        def final(n):
            at = pl.ds(n, 16)
            whole = (g[rows(r[h], q[h], n, 16), cols[h]].astype(F32) + p2[h, at].astype(F32)
                     + pf[h, at].astype(F32) + nz[h, at])
            fin[h, at] = (whole * (1.0 / 16.0)).astype(BF16)

        strips(piece, final)
        mine = out_hbm.at[rows(r[h], q[h]), cols[h]]
        remote(fin.at[h], mine, ag1_send.at[h], ag1_recv.at[h, 0], r_up[h])
        remote(fin.at[h], mine, ag1_send.at[h], ag1_recv.at[h, 1], r_down[h])
        remote(fin.at[h], mine, ag2_send.at[h, 0], ag2_recv.at[h, r[h], 0], q_up[h])
        remote(fin.at[h], mine, ag2_send.at[h, 0], ag2_recv.at[h, r[h], 1], q_down[h])
        pltpu.make_async_copy(fin.at[h], mine, own_sem.at[h]).start()

    def place(h, b, p, start=0, size=None):
        return out_hbm.at[rows(b, p, start, size), cols[h]]

    def spread(h, away):
        b = turn(r[h], away)
        at = place(h, b, q[h])
        remote(at, at, ag2_send.at[h, away], ag2_recv.at[h, b, 0], q_up[h])
        remote(at, at, ag2_send.at[h, away], ag2_recv.at[h, b, 1], q_down[h])

    for h in range(2):
        b = turn(r[h], -1)
        await_bytes(place(h, b, q[h]), ag1_recv.at[h, 0])
        at = place(h, b, q[h], 0, up)
        remote(at, at, ag1_send.at[h], ag1_recv.at[h, 2], r_up[h])
        b = turn(r[h], 1)
        await_bytes(place(h, b, q[h]), ag1_recv.at[h, 1])
        at = place(h, b, q[h], up, down)
        remote(at, at, ag1_send.at[h], ag1_recv.at[h, 2], r_down[h])
        spread(h, 3)
        spread(h, 1)

    def relay(h, away):
        b = turn(r[h], away)
        p = turn(q[h], -1)
        await_bytes(place(h, b, p), ag2_recv.at[h, b, 0])
        at = place(h, b, p, 0, up)
        remote(at, at, ag2_send.at[h, away], ag2_recv.at[h, b, 2], q_up[h])
        p = turn(q[h], 1)
        await_bytes(place(h, b, p), ag2_recv.at[h, b, 1])
        at = place(h, b, p, up, down)
        remote(at, at, ag2_send.at[h, away], ag2_recv.at[h, b, 2], q_down[h])

    for h in range(2):
        relay(h, 0)
    for h in range(2):
        b = turn(r[h], 2)
        await_bytes(place(h, b, q[h]), ag1_recv.at[h, 2])
        spread(h, 2)
    for away in (3, 1, 2):
        for h in range(2):
            relay(h, away)
    for away in (0, 3, 1, 2):
        for h in range(2):
            b = turn(r[h], away)
            await_bytes(place(h, b, turn(q[h], 2)), ag2_recv.at[h, b, 2])

    for h in range(2):
        await_bytes(g.at[pl.ds(0, 3 * piece), cols[0]], p_send.at[h])
        await_bytes(g.at[pl.ds(0, 3 * piece), cols[0]], ag1_send.at[h])
        await_bytes(fin.at[h], own_sem.at[h])
        for b in range(RING):
            await_bytes(g.at[pl.ds(0, 2 * piece), cols[0]], raw_send.at[h, b])
            await_bytes(g.at[pl.ds(0, piece), cols[0]], fw_send.at[h, b])
            await_bytes(g.at[pl.ds(0, 3 * piece), cols[0]], ag2_send.at[h, b])
    for side in range(2):
        for m in (4, 5):
            await_bytes(ot_v.at[pl.ds(0, piece)], x_send.at[side, m])
    await_bytes(nrm.at[pl.ds(0, 7)], nrm_send)
    await_bytes(fac.at[pl.ds(1, 4)], fac_send)

    @pl.when(z != y)
    def _():
        await_bytes(nz.at[0], nz_send)


def on_device(hidden, out_grad, lengths, noise):
    _, _, seq_len, units = hidden.shape
    block = out_grad.shape[3]
    width = block * lax.axis_size("tensor")
    layers = lax.axis_size("layer")
    bound = float((seq_len * layers * units * lax.axis_size("tensor") * width / 64.0) ** 0.5)
    positions = lax.broadcasted_iota(jnp.int32, (seq_len, 1), 0)
    valid = positions < lengths[0]
    turned = jnp.where(valid, out_grad[0, 0], jnp.zeros((), BF16)).T
    piece, half = block // RING, units // 2
    dma = pltpu.SemaphoreType.DMA
    result = pl.pallas_call(
        functools.partial(kernel, bound),
        out_shape=jax.ShapeDtypeStruct((width, units), BF16),
        in_specs=[pl.BlockSpec(memory_space=pl.ANY)] * 3,
        out_specs=pl.BlockSpec(memory_space=pl.ANY),
        scratch_shapes=[
            pltpu.VMEM((seq_len, units), BF16),
            pltpu.VMEM((width, seq_len), BF16),
            pltpu.VMEM((width, units), BF16),
            pltpu.VMEM((2, RING, piece, half), BF16),
            pltpu.VMEM((2, RING, piece, half), BF16),
            pltpu.VMEM((2, RING, piece, half), BF16),
            pltpu.VMEM((2, piece, half), BF16),
            pltpu.VMEM((2, piece, half), BF16),
            pltpu.VMEM((2, piece, half), BF16),
            pltpu.VMEM((2, piece, half), F32),
            pltpu.VMEM((2, piece, half), BF16),
            pltpu.VMEM((8, 256), F32),
            pltpu.VMEM((2 * RING, 8, 128), F32),
            pltpu.VMEM((5, 8, 128), F32),
            dma((3,)), dma((2, 6)), dma((2, 6)),
            dma((2, RING)), dma((2, RING)), dma((2, RING)), dma((2, RING)), dma((2, RING)),
            dma((2,)), dma((2,)), dma((2,)), dma((2,)),
            dma, dma, dma, dma, dma, dma,
            dma((2,)), dma((2, 3)), dma((2, RING)), dma((2, RING, 3)), dma((2,)),
        ],
        compiler_params=pltpu.CompilerParams(
            collective_id=0, has_side_effects=True, vmem_limit_bytes=56 * 1024 * 1024
        ),
        cost_estimate=pl.CostEstimate(
            flops=2 * width * units * seq_len, bytes_accessed=30_000_000, transcendentals=0
        ),
    )(turned, hidden[0, 0], noise[0])
    return result[None]


def solution(mesh):
    placed = (
        P("layer", "dp", None, "tensor"),
        P("layer", "dp", None, "tensor"),
        P("dp"),
        P("layer", "dp", "tensor"),
    )
    return jax.shard_map(
        on_device, mesh=mesh, in_specs=placed, out_specs=P("layer", None, "tensor"), check_vma=False
    )
```

time: 322 us -> 167 us (0.52)
  waiting for transfers between devices: 225 us -> 0 us
  Pallas kernels: 0 us -> 154 us
  matrix products: 35.9 us -> 0 us
  local copies, waits for them, and re-layouts: 30.3 us -> 9.84 us
  between operations: 14.5 us -> 0.67 us
  blocking collectives: 13.5 us -> 0 us
    pallas_call x0 -> x1, Pallas kernels: none -> 154 us  [on_device(): pl.pallas_call(functools.partial(kernel, bound), out_shape=jax.ShapeDtype...]
    all_gather x2 -> x0, waiting for transfers between devices: 137 us -> none  [the longest x1 80.5 us: on_device(): whole = lax.all_gather(noised, 'dp', axis=0, tiled=True)]
    unnamed x4 -> x0, waiting for transfers between devices: 88.5 us -> none
    dot_general x3 -> x0, matrix products: 35.9 us -> none  [the longest x1 17.6 us: on_device(): jnp.einsum('stk,stf->skf', grads_full, kept, preferred_element_type=jnp.f...]
    unnamed x4 -> x1, local copies, waits for them, and re-layouts: 28.1 us -> 9.84 us
    psum x1 -> x0, blocking collectives: 13.5 us -> none  [on_device(): squares = lax.psum(partial_sq, ('tensor', 'layer'))]
  transfers between devices with their start and end apart: 3 -> 0, of which waited for: 3 -> 0; matrix products, arithmetic and copies ran while one was open for 1% -> 0% of each run, Pallas kernels for 0% -> 0%
where the time goes in v1:
time: 167 us
  Pallas kernels  154 us (92%)
  local copies, waits for them, and re-layouts  9.84 us (6%)
  other arithmetic  2.37 us (1%)
    pallas_call x1, Pallas kernels, on_device(): pl.pallas_call(functools.partial(kernel, bound), out_shape=jax.ShapeDtype...  154 us
    unnamed x1, local copies, waits for them, and re-layouts  9.84 us

profile of v1, /device:TPU:0, one launch (start us, length us, event | category | flops | bytes accessed | tf_op | source)
XLA Modules:
  0.0 166.7 jit_solution(1108486300291351236)
XLA Ops:
  0.7 2.4 %fusion.ot_hbm = bf16[576,1024]{1,0:T(8,128)(2,1)} fusion(bf16[1,1,1024,576]{2,3,1,0:T(8,128)(2,1)} %param.5, pred[1024]{0:T(1024)(128)(4,1)S(1)} %iota_compare_fusion), kind=kLoop, calls=%fused_computation.1 | loop fusion | flops 589824 | bytes 2360320 | tf_op jit(solution)/shard_map/transpose | solution.py:353
  3.0 153.8 %shard_map.46 = bf16[2304,2304]{1,0:T(8,128)(2,1)} custom-call(bf16[576,1024]{1,0:T(8,128)(2,1)} %fusion.ot_hbm, bf16[1024,2304]{1,0:T(8,128)(2,1)} %bitcast.12, f32[144,2304]{1,0:T(8,128)} %bitcast.13), custom_call_target="tpu_custom_call" | custom-call | flops 10871635968 | bytes 30000000 | tf_op jit(solution)/shard_map/pallas_call | solution.py:356
  156.8 9.8 %copy.7 = bf16[1,2304,2304]{2,1,0:T(8,128)(2,1)} copy(bf16[1,2304,2304]{2,1,0:T(8,128)(2,1)} %bitcast.11) | data formatting | bytes 21233664
  (1 shorter events, 0.0 us)

commit v2 on v1

v2 whole, which is shorter than its diff:
```python
import functools

import jax
import jax.numpy as jnp
from jax import lax
from jax.experimental import pallas as pl
from jax.experimental.pallas import tpu as pltpu
from jax.sharding import PartitionSpec as P

MESH = pl.DeviceIdType.MESH
RING = 4
F32 = jnp.float32
BF16 = jnp.bfloat16


def kernel(bound, len_ref, o_hbm, h_hbm, noise_hbm, out,
           h_v, ot_v, g, r1, r2, fw, p1, p2, pf, nz, sq, nrm, fac,
           load_sem, x_send, x_recv, raw_send, r1_recv, r2_recv, fw_send, fw_recv,
           p_send, p1_recv, p2_recv, pf_recv, nrm_send, nrm_recv,
           fac_send, fac_recv, ag1_send, ag1_recv, ag2_send, ag2_recv):
    dp = lax.axis_index("dp")
    x = lax.axis_index("tensor")
    core = lax.axis_index("layer")
    z, y = dp // RING, dp % RING
    block, tokens = o_hbm.shape
    units = h_hbm.shape[1]
    piece = block // RING
    half = units // 2
    up = (piece // 32) * 16 + 16 * (piece // 16 % 2)
    down = piece - up

    def turn(i, by):
        return (i + by + RING) % RING

    z_up, z_down = {"dp": turn(z, 1) * RING + y}, {"dp": turn(z, -1) * RING + y}
    y_up, y_down = {"dp": z * RING + turn(y, 1)}, {"dp": z * RING + turn(y, -1)}
    x_up, x_down = {"tensor": turn(x, 1)}, {"tensor": turn(x, -1)}
    q, r = (z, y), (y, z)
    q_up, q_down = (z_up, y_up), (z_down, y_down)
    r_up, r_down = (y_up, z_up), (y_down, z_down)
    cols = (pl.ds(0, half), pl.ds(half, half))

    def rows(b, p, start=0, size=None):
        return pl.ds(pl.multiple_of(b * block + p * piece + start, 16), piece if size is None else size)

    def chunk(h, u, v, start=0, size=None):
        return rows(u, v, start, size) if h == 0 else rows(v, u, start, size)

    def remote(src, dst, send, recv, device):
        pltpu.make_async_remote_copy(src_ref=src, dst_ref=dst, send_sem=send, recv_sem=recv,
                                     device_id=device, device_id_type=MESH).start()

    def await_bytes(ref, sem):
        pltpu.make_async_copy(ref, ref, sem).wait()

    me = x * 2 + core
    group = []
    for k in range(1, 2 * RING):
        other = (me + k) % (2 * RING)
        group.append({"tensor": other // 2, "layer": other % 2})

    own = pl.multiple_of(x * block, 16)
    load_o = pltpu.make_async_copy(o_hbm, ot_v.at[pl.ds(own, block)], load_sem.at[1])
    load_o.start()
    load_h = pltpu.make_async_copy(h_hbm, h_v, load_sem.at[0])
    load_h.start()
    load_n = pltpu.make_async_copy(noise_hbm, nz, load_sem.at[2])
    load_n.start()

    barrier = pltpu.get_barrier_semaphore()
    for device in group + [z_up, z_down, y_up, y_down]:
        pl.semaphore_signal(barrier, inc=1, device_id=device, device_id_type=MESH)

    pl.semaphore_wait(barrier, 11)

    def passed_on(m):
        return (m == 2) | (m == 4)

    def first(m):
        return jnp.where(m < 2, m, jnp.where(m < 4, jnp.where(m == 2, 0, 2), jnp.where(m == 4, 1, 3)))

    def x_start_up(m):
        at = ot_v.at[rows(jnp.where(passed_on(m), turn(x, -1), x), first(m))]
        remote(at, at, x_send.at[0, m], x_recv.at[0, m], x_up)

    def x_start_down(m):
        at = ot_v.at[rows(jnp.where(passed_on(m), turn(x, 1), x), (first(m) + 2) % RING)]
        remote(at, at, x_send.at[1, m], x_recv.at[1, m], x_down)

    load_o.wait()
    kept = lax.broadcasted_iota(jnp.int32, (16, tokens), 1) < len_ref[0]
    for p in (0, 2, 1, 3):
        @pl.loop(0, piece // 16)
        def _(n):
            at = rows(x, p, n * 16, 16)
            ot_v[at] = jnp.where(kept, ot_v[at], jnp.zeros((), BF16))

        if p < 2:
            x_start_up(jnp.int32(p))
        else:
            x_start_down(jnp.int32(p - 2))

    sq[...] = jnp.zeros_like(sq)
    load_h.wait()

    def product(ba, pa, bb, pb):
        wide = sq.shape[1]

        @pl.loop(0, units // wide)
        def _(n):
            at = pl.ds(pl.multiple_of(n * wide, wide), wide)
            left = jnp.concatenate([ot_v[rows(ba, pa)], ot_v[rows(bb, pb)]], axis=0)
            out = jnp.dot(left, h_v[:, at], preferred_element_type=F32)
            sq[...] += jnp.sum((out * out).reshape(2 * piece // 8, 8, wide), axis=0)
            low = out.astype(BF16)
            g[rows(ba, pa), at] = low[:piece]
            g[rows(bb, pb), at] = low[piece:]

    def send_raw(b, p):
        for h in range(2):
            u, v = (b, p) if h == 0 else (p, b)
            away = turn(u - q[h], 0)
            upper = g.at[rows(b, p, 0, up), cols[h]]
            lower = g.at[rows(b, p, up, down), cols[h]]

            @pl.when(away == 1)
            def _():
                remote(lower, r2.at[h, v, pl.ds(up, down)], raw_send.at[h, v], r2_recv.at[h, v], q_up[h])

            @pl.when(away == 2)
            def _():
                remote(upper, r1.at[h, v, pl.ds(0, up)], raw_send.at[h, v], r1_recv.at[h, v], q_up[h])
                remote(lower, r1.at[h, v, pl.ds(up, down)], raw_send.at[h, v], r1_recv.at[h, v], q_down[h])

            @pl.when(away == 3)
            def _():
                remote(upper, r2.at[h, v, pl.ds(0, up)], raw_send.at[h, v], r2_recv.at[h, v], q_down[h])

    @pl.loop(0, 2)
    def _(i):
        product(x, 2 * i, x, 2 * i + 1)
        send_raw(x, 2 * i)
        send_raw(x, 2 * i + 1)

    @pl.loop(0, 6)
    def _(i):
        ba, pa = jnp.where(passed_on(i), turn(x, 2), turn(x, -1)), first(i)
        bb, pb = jnp.where(passed_on(i), turn(x, 2), turn(x, 1)), (first(i) + 2) % RING
        await_bytes(ot_v.at[rows(ba, pa)], x_recv.at[0, i])
        await_bytes(ot_v.at[rows(bb, pb)], x_recv.at[1, i])

        @pl.when(i < 4)
        def _():
            await_bytes(ot_v.at[pl.ds(0, piece)], x_send.at[0, i])
            await_bytes(ot_v.at[pl.ds(0, piece)], x_send.at[1, i])
            x_start_up(i + 2)
            x_start_down(i + 2)

        product(ba, pa, bb, pb)
        send_raw(ba, pa)
        send_raw(bb, pb)

    nrm[pl.ds(me, 1)] = (sq[:, :128] + sq[:, 128:])[None]
    for device in group:
        remote(nrm.at[me], nrm.at[me], nrm_send, nrm_recv, device)
    await_bytes(nrm.at[pl.ds(0, 7)], nrm_recv)
    total = jnp.sum(jnp.sum(nrm[...], axis=0), keepdims=True)
    factor = jnp.minimum(jnp.float32(1.0), bound / jnp.sqrt(total + 1e-06))
    fac[0] = jnp.broadcast_to(factor, fac.shape[1:])
    for slot, device in ((1, z_up), (2, z_down), (3, y_up), (4, y_down)):
        remote(fac.at[0], fac.at[slot], fac_send, fac_recv, device)
    await_bytes(fac.at[pl.ds(1, 4)], fac_recv)
    scale = fac[0, 0:1, 0:1]
    before = (fac[1, 0:1, 0:1], fac[3, 0:1, 0:1])
    after = (fac[2, 0:1, 0:1], fac[4, 0:1, 0:1])

    def strips(size, body):
        @pl.loop(0, size // 16)
        def _(n):
            body(pl.multiple_of(n * 16, 16))

    def away_of(i):
        return jnp.where(i == 0, 2, jnp.where(i == 1, 1, jnp.where(i == 2, 3, 0)))

    @pl.loop(0, RING)
    def _(i):
        for h in range(2):
            v = turn(r[h], away_of(i))
            await_bytes(r1.at[h, v], r1_recv.at[h, v])

            def upper(n):
                at = chunk(h, turn(q[h], 1), v, n, 16)
                g[at, cols[h]] = (scale * g[at, cols[h]].astype(F32)
                                  + before[h] * r1[h, v, pl.ds(n, 16)].astype(F32)).astype(BF16)

            strips(up, upper)
            remote(g.at[chunk(h, turn(q[h], 1), v, 0, up), cols[h]], fw.at[h, v, pl.ds(0, up)],
                   fw_send.at[h, v], fw_recv.at[h, v], q_up[h])

            def lower(n):
                at = chunk(h, turn(q[h], -1), v, up + n, 16)
                g[at, cols[h]] = (scale * g[at, cols[h]].astype(F32)
                                  + after[h] * r1[h, v, pl.ds(up + n, 16)].astype(F32)).astype(BF16)

            strips(down, lower)
            remote(g.at[chunk(h, turn(q[h], -1), v, up, down), cols[h]], fw.at[h, v, pl.ds(up, down)],
                   fw_send.at[h, v], fw_recv.at[h, v], q_down[h])

    @pl.loop(0, RING)
    def _(i):
        away = away_of(i)
        for h in range(2):
            v = turn(r[h], away)
            await_bytes(r2.at[h, v], r2_recv.at[h, v])
            await_bytes(fw.at[h, v], fw_recv.at[h, v])

            def gathered(other, start):
                def body(n):
                    n = start + n
                    at = chunk(h, q[h], v, n, 16)
                    g[at, cols[h]] = (scale * g[at, cols[h]].astype(F32)
                                      + fw[h, v, pl.ds(n, 16)].astype(F32)
                                      + other * r2[h, v, pl.ds(n, 16)].astype(F32)).astype(BF16)
                return body

            strips(up, gathered(after[h], 0))
            strips(down, gathered(before[h], up))
            upper = g.at[chunk(h, q[h], v, 0, up), cols[h]]
            lower = g.at[chunk(h, q[h], v, up, down), cols[h]]

            @pl.when(away == 1)
            def _():
                remote(lower, p2.at[h, pl.ds(up, down)], p_send.at[h], p2_recv.at[h], r_up[h])

            @pl.when(away == 2)
            def _():
                remote(upper, p1.at[h, pl.ds(0, up)], p_send.at[h], p1_recv.at[h], r_up[h])
                remote(lower, p1.at[h, pl.ds(up, down)], p_send.at[h], p1_recv.at[h], r_down[h])

            @pl.when(away == 3)
            def _():
                remote(upper, p2.at[h, pl.ds(0, up)], p_send.at[h], p2_recv.at[h], r_down[h])

    for h in range(2):
        await_bytes(p1.at[h], p1_recv.at[h])

        def upper(n):
            at = chunk(h, q[h], turn(r[h], 1), n, 16)
            g[at, cols[h]] = (g[at, cols[h]].astype(F32) + p1[h, pl.ds(n, 16)].astype(F32)).astype(BF16)

        strips(up, upper)
        remote(g.at[chunk(h, q[h], turn(r[h], 1), 0, up), cols[h]], pf.at[h, pl.ds(0, up)],
               p_send.at[h], pf_recv.at[h], r_up[h])

        def lower(n):
            at = chunk(h, q[h], turn(r[h], -1), up + n, 16)
            g[at, cols[h]] = (g[at, cols[h]].astype(F32) + p1[h, pl.ds(up + n, 16)].astype(F32)).astype(BF16)

        strips(down, lower)
        remote(g.at[chunk(h, q[h], turn(r[h], -1), up, down), cols[h]], pf.at[h, pl.ds(up, down)],
               p_send.at[h], pf_recv.at[h], r_down[h])

    def place(h, u, v, start=0, size=None):
        return out.at[chunk(h, u, v, start, size), cols[h]]

    def spread(h, away):
        v = turn(r[h], away)
        at = place(h, q[h], v)
        remote(at, at, ag2_send.at[h, away], ag2_recv.at[h, v, 0], q_up[h])
        remote(at, at, ag2_send.at[h, away], ag2_recv.at[h, v, 1], q_down[h])

    load_n.wait()
    for h in range(2):
        await_bytes(p2.at[h], p2_recv.at[h])
        await_bytes(pf.at[h], pf_recv.at[h])

        def final(n):
            at = pl.ds(n, 16)
            whole = (g[chunk(h, q[h], r[h], n, 16), cols[h]].astype(F32) + p2[h, at].astype(F32)
                     + pf[h, at].astype(F32) + nz[at, cols[h]])
            out[chunk(h, q[h], r[h], n, 16), cols[h]] = (whole * (1.0 / 16.0)).astype(BF16)

        strips(piece, final)
        mine = place(h, q[h], r[h])
        remote(mine, mine, ag1_send.at[h], ag1_recv.at[h, 0], r_up[h])
        remote(mine, mine, ag1_send.at[h], ag1_recv.at[h, 1], r_down[h])
        spread(h, 0)

    for h in range(2):
        v = turn(r[h], -1)
        await_bytes(place(h, q[h], v), ag1_recv.at[h, 0])
        at = place(h, q[h], v, 0, up)
        remote(at, at, ag1_send.at[h], ag1_recv.at[h, 2], r_up[h])
        v = turn(r[h], 1)
        await_bytes(place(h, q[h], v), ag1_recv.at[h, 1])
        at = place(h, q[h], v, up, down)
        remote(at, at, ag1_send.at[h], ag1_recv.at[h, 2], r_down[h])
        spread(h, 3)
        spread(h, 1)

    def relay(h, away):
        v = turn(r[h], away)
        u = turn(q[h], -1)
        await_bytes(place(h, u, v), ag2_recv.at[h, v, 0])
        at = place(h, u, v, 0, up)
        remote(at, at, ag2_send.at[h, away], ag2_recv.at[h, v, 2], q_up[h])
        u = turn(q[h], 1)
        await_bytes(place(h, u, v), ag2_recv.at[h, v, 1])
        at = place(h, u, v, up, down)
        remote(at, at, ag2_send.at[h, away], ag2_recv.at[h, v, 2], q_down[h])

    for h in range(2):
        relay(h, 0)
    for h in range(2):
        v = turn(r[h], 2)
        await_bytes(place(h, q[h], v), ag1_recv.at[h, 2])
        spread(h, 2)
    for away in (3, 1, 2):
        for h in range(2):
            relay(h, away)
    for away in (0, 3, 1, 2):
        for h in range(2):
            v = turn(r[h], away)
            await_bytes(place(h, turn(q[h], 2), v), ag2_recv.at[h, v, 2])

    for h in range(2):
        await_bytes(g.at[pl.ds(0, 3 * piece), cols[0]], p_send.at[h])
        await_bytes(g.at[pl.ds(0, 3 * piece), cols[0]], ag1_send.at[h])
        for b in range(RING):
            await_bytes(g.at[pl.ds(0, 2 * piece), cols[0]], raw_send.at[h, b])
            await_bytes(g.at[pl.ds(0, piece), cols[0]], fw_send.at[h, b])
            await_bytes(g.at[pl.ds(0, 3 * piece), cols[0]], ag2_send.at[h, b])
    for side in range(2):
        for m in (4, 5):
            await_bytes(ot_v.at[pl.ds(0, piece)], x_send.at[side, m])
    await_bytes(nrm.at[pl.ds(0, 7)], nrm_send)
    await_bytes(fac.at[pl.ds(1, 4)], fac_send)


def on_device(hidden, out_grad, lengths, noise):
    _, _, seq_len, units = hidden.shape
    block = out_grad.shape[3]
    width = block * lax.axis_size("tensor")
    layers = lax.axis_size("layer")
    bound = float((seq_len * layers * units * lax.axis_size("tensor") * width / 64.0) ** 0.5)
    piece, half = block // RING, units // 2
    dma = pltpu.SemaphoreType.DMA
    result = pl.pallas_call(
        functools.partial(kernel, bound),
        out_shape=pltpu.VMEM((width, units), BF16),
        in_specs=[pl.BlockSpec(memory_space=pltpu.SMEM)] + [pl.BlockSpec(memory_space=pltpu.HBM)] * 3,
        out_specs=pl.BlockSpec(memory_space=pltpu.VMEM),
        scratch_shapes=[
            pltpu.VMEM((seq_len, units), BF16),
            pltpu.VMEM((width, seq_len), BF16),
            pltpu.VMEM((width, units), BF16),
            pltpu.VMEM((2, RING, piece, half), BF16),
            pltpu.VMEM((2, RING, piece, half), BF16),
            pltpu.VMEM((2, RING, piece, half), BF16),
            pltpu.VMEM((2, piece, half), BF16),
            pltpu.VMEM((2, piece, half), BF16),
            pltpu.VMEM((2, piece, half), BF16),
            pltpu.VMEM((piece, units), F32),
            pltpu.VMEM((8, 256), F32),
            pltpu.VMEM((2 * RING, 8, 128), F32),
            pltpu.VMEM((5, 8, 128), F32),
            dma((3,)), dma((2, 6)), dma((2, 6)),
            dma((2, RING)), dma((2, RING)), dma((2, RING)), dma((2, RING)), dma((2, RING)),
            dma((2,)), dma((2,)), dma((2,)), dma((2,)),
            dma, dma, dma, dma,
            dma((2,)), dma((2, 3)), dma((2, RING)), dma((2, RING, 3)),
        ],
        compiler_params=pltpu.CompilerParams(
            collective_id=0, has_side_effects=True, vmem_limit_bytes=40 * 1024 * 1024
        ),
        cost_estimate=pl.CostEstimate(
            flops=2 * width * units * seq_len, bytes_accessed=30_000_000, transcendentals=0
        ),
    )(lengths, *(pltpu.with_memory_space_constraint(a, pltpu.HBM) for a in (out_grad[0, 0].T, hidden[0, 0], noise[0])))
    return result[None]


def solution(mesh):
    placed = (
        P("layer", "dp", None, "tensor"),
        P("layer", "dp", None, "tensor"),
        P("dp"),
        P("layer", "dp", "tensor"),
    )
    return jax.shard_map(
        on_device, mesh=mesh, in_specs=placed, out_specs=P("layer", None, "tensor"), check_vma=False
    )
```

time: 167 us -> 149 us (0.89)
  Pallas kernels: 154 us -> 144 us
  local copies, waits for them, and re-layouts: 9.84 us -> 4.13 us
  other arithmetic: 2.37 us -> 0 us
    pallas_call x1, Pallas kernels: 154 us -> 144 us  [on_device(): pl.pallas_call(functools.partial(kernel, bound), out_shape=pltpu.VMEM((wi...]
    unnamed x1, local copies, waits for them, and re-layouts: 9.84 us -> 4.13 us
    transpose x1 -> x0, other arithmetic: 2.37 us -> none  [on_device(): turned = jnp.where(valid, out_grad[0, 0], jnp.zeros((), BF16)).T]
where the time goes in v2:
time: 149 us
  Pallas kernels  144 us (97%)
  local copies, waits for them, and re-layouts  4.13 us (3%)
    pallas_call x1, Pallas kernels, on_device(): pl.pallas_call(functools.partial(kernel, bound), out_shape=pltpu.VMEM((wi...  144 us
    unnamed x1, local copies, waits for them, and re-layouts  4.13 us

profile of v2, /device:TPU:0, one launch (start us, length us, event | category | flops | bytes accessed | tf_op | source)
XLA Modules:
  0.0 148.9 jit_solution(7645486680197993095)
XLA Ops:
  0.7 144.1 %shard_map.46 = bf16[2304,2304]{1,0:T(8,128)(2,1)S(1)} custom-call(s32[1]{0:T(128)S(6)} %copy.7.len_ref, bf16[576,1024]{1,0:T(8,128)(2,1)} %bitcast.9, bf16[1024,2304]{1,0:T(8,128)(2,1)} %bitcast.7, f32[144,2304]{1,0:T(8,128)} %bitcast.8), custom_call_target="tpu_custom_call" | custom-call | flops 10871635968 | bytes 30000000 | tf_op jit(solution)/shard_map/pallas_call | solution.py:348
  144.8 4.1 %copy.6 = bf16[1,2304,2304]{2,1,0:T(8,128)(2,1)} copy(bf16[1,2304,2304]{2,1,0:T(8,128)(2,1)S(1)} %bitcast.6) | data formatting | bytes 21233664

commit v3 on v2

--- a/solution.py
+++ b/solution.py
@@ -14,7 +14,7 @@
 
 
 def kernel(bound, len_ref, o_hbm, h_hbm, noise_hbm, out,
-           h_v, ot_v, g, r1, r2, fw, p1, p2, pf, nz, sq, nrm, fac,
+           h_v, ot_v, g, r1, from_down, from_up, fw, p1, p2, pf, nz, sq, nrm, fac,
            load_sem, x_send, x_recv, raw_send, r1_recv, r2_recv, fw_send, fw_recv,
            p_send, p1_recv, p2_recv, pf_recv, nrm_send, nrm_recv,
            fac_send, fac_recv, ag1_send, ag1_recv, ag2_send, ag2_recv):
@@ -26,8 +26,7 @@
     units = h_hbm.shape[1]
     piece = block // RING
     half = units // 2
-    up = (piece // 32) * 16 + 16 * (piece // 16 % 2)
-    down = piece - up
+    cuts = (piece - piece // 32 * 16, piece // 32 * 16)
 
     def turn(i, by):
         return (i + by + RING) % RING
@@ -35,8 +34,9 @@
     z_up, z_down = {"dp": turn(z, 1) * RING + y}, {"dp": turn(z, -1) * RING + y}
     y_up, y_down = {"dp": z * RING + turn(y, 1)}, {"dp": z * RING + turn(y, -1)}
     x_up, x_down = {"tensor": turn(x, 1)}, {"tensor": turn(x, -1)}
+    z_far, y_far = {"dp": turn(z, 2) * RING + y}, {"dp": z * RING + turn(y, 2)}
     q, r = (z, y), (y, z)
-    q_up, q_down = (z_up, y_up), (z_down, y_down)
+    q_up, q_down, q_far = (z_up, y_up), (z_down, y_down), (z_far, y_far)
     r_up, r_down = (y_up, z_up), (y_down, z_down)
     cols = (pl.ds(0, half), pl.ds(half, half))
 
@@ -68,16 +68,16 @@
     load_n.start()
 
     barrier = pltpu.get_barrier_semaphore()
-    for device in group + [z_up, z_down, y_up, y_down]:
+    for device in group + [z_up, z_down, z_far, y_up, y_down, y_far]:
         pl.semaphore_signal(barrier, inc=1, device_id=device, device_id_type=MESH)
 
-    pl.semaphore_wait(barrier, 11)
+    pl.semaphore_wait(barrier, 13)
 
     def passed_on(m):
-        return (m == 2) | (m == 4)
+        return (m == 2) | (m == 5)
 
     def first(m):
-        return jnp.where(m < 2, m, jnp.where(m < 4, jnp.where(m == 2, 0, 2), jnp.where(m == 4, 1, 3)))
+        return jnp.where((m == 0) | (m == 2), 0, jnp.where(m == 1, 2, jnp.where(m == 4, 3, 1)))
 
     def x_start_up(m):
         at = ot_v.at[rows(jnp.where(passed_on(m), turn(x, -1), x), first(m))]
@@ -95,52 +95,76 @@
             at = rows(x, p, n * 16, 16)
             ot_v[at] = jnp.where(kept, ot_v[at], jnp.zeros((), BF16))
 
-        if p < 2:
-            x_start_up(jnp.int32(p))
-        else:
-            x_start_down(jnp.int32(p - 2))
+        if p == 2:
+            for m in range(2):
+                x_start_up(jnp.int32(m))
+                x_start_down(jnp.int32(m))
 
     sq[...] = jnp.zeros_like(sq)
     load_h.wait()
 
+    def kind(h, b, p):
+        if h == 0:
+            return p // 2, p % 2 == 0
+        ahead = turn(b - x, 0)
+        return ahead // 2, (ahead == 0) | (ahead == 3)
+
+    def send_raw(h, b, p):
+        u, v = (b, p) if h == 0 else (p, b)
+        away = turn(u - q[h], 0)
+        cut, direct = kind(h, b, p)
+        whole = g.at[rows(b, p), cols[h]]
+
+        @pl.when(direct & (away == 1))
+        def _():
+            remote(whole, from_down.at[h, v], raw_send.at[h, v], r2_recv.at[h, v], q_up[h])
+
+        @pl.when(direct & (away == 3))
+        def _():
+            remote(whole, from_up.at[h, v], raw_send.at[h, v], r2_recv.at[h, v], q_down[h])
+
+        for k, up in enumerate(cuts):
+            upper, lower = g.at[rows(b, p, 0, up), cols[h]], g.at[rows(b, p, up, piece - up), cols[h]]
+            above, below = pl.ds(0, up), pl.ds(up, piece - up)
+
+            @pl.when((cut == k) & ~direct & (away == 1))
+            def _():
+                remote(lower, from_down.at[h, v, below], raw_send.at[h, v], r2_recv.at[h, v], q_up[h])
+
+            @pl.when((cut == k) & ~direct & (away == 3))
+            def _():
+                remote(upper, from_up.at[h, v, above], raw_send.at[h, v], r2_recv.at[h, v], q_down[h])
+
+            @pl.when((cut == k) & (away == 2))
+            def _():
+                remote(upper, r1.at[h, v, above], raw_send.at[h, v], r1_recv.at[h, v], q_up[h])
+                remote(lower, r1.at[h, v, below], raw_send.at[h, v], r1_recv.at[h, v], q_down[h])
+
     def product(ba, pa, bb, pb):
-        wide = sq.shape[1]
-
-        @pl.loop(0, units // wide)
-        def _(n):
-            at = pl.ds(pl.multiple_of(n * wide, wide), wide)
+        for h in range(2):
             left = jnp.concatenate([ot_v[rows(ba, pa)], ot_v[rows(bb, pb)]], axis=0)
-            out = jnp.dot(left, h_v[:, at], preferred_element_type=F32)
-            sq[...] += jnp.sum((out * out).reshape(2 * piece // 8, 8, wide), axis=0)
-            low = out.astype(BF16)
-            g[rows(ba, pa), at] = low[:piece]
-            g[rows(bb, pb), at] = low[piece:]
-
-    def send_raw(b, p):
-        for h in range(2):
-            u, v = (b, p) if h == 0 else (p, b)
-            away = turn(u - q[h], 0)
-            upper = g.at[rows(b, p, 0, up), cols[h]]
-            lower = g.at[rows(b, p, up, down), cols[h]]
-
-            @pl.when(away == 1)
-            def _():
-                remote(lower, r2.at[h, v, pl.ds(up, down)], raw_send.at[h, v], r2_recv.at[h, v], q_up[h])
-
-            @pl.when(away == 2)
-            def _():
-                remote(upper, r1.at[h, v, pl.ds(0, up)], raw_send.at[h, v], r1_recv.at[h, v], q_up[h])
-                remote(lower, r1.at[h, v, pl.ds(up, down)], raw_send.at[h, v], r1_recv.at[h, v], q_down[h])
-
-            @pl.when(away == 3)
-            def _():
-                remote(upper, r2.at[h, v, pl.ds(0, up)], raw_send.at[h, v], r2_recv.at[h, v], q_down[h])
+            result = jnp.dot(left, h_v[:, cols[h]], preferred_element_type=F32)
+            sq[...] += jnp.sum((result * result).reshape(2 * piece // 8, 8, half), axis=0)
+            low = result.astype(BF16)
+            g[rows(ba, pa), cols[h]] = low[:piece]
+            g[rows(bb, pb), cols[h]] = low[piece:]
+            send_raw(h, ba, pa)
+            send_raw(h, bb, pb)
+
+    def second(h, rel):
+        return rel if h == 0 else turn(x, rel)
+
+    def relay_raw(h, rel):
+        v = second(h, rel)
+        up = cuts[rel // 2]
+        await_bytes(r1.at[h, v], r1_recv.at[h, v])
+        remote(r1.at[h, v, pl.ds(0, up)], fw.at[h, v, pl.ds(0, up)], fw_send.at[h, v], fw_recv.at[h, v], q_up[h])
+        remote(r1.at[h, v, pl.ds(up, piece - up)], fw.at[h, v, pl.ds(up, piece - up)],
+               fw_send.at[h, v], fw_recv.at[h, v], q_down[h])
 
     @pl.loop(0, 2)
     def _(i):
         product(x, 2 * i, x, 2 * i + 1)
-        send_raw(x, 2 * i)
-        send_raw(x, 2 * i + 1)
 
     @pl.loop(0, 6)
     def _(i):
@@ -157,90 +181,119 @@
             x_start_down(i + 2)
 
         product(ba, pa, bb, pb)
-        send_raw(ba, pa)
-        send_raw(bb, pb)
-
-    nrm[pl.ds(me, 1)] = (sq[:, :128] + sq[:, 128:])[None]
+
+        @pl.when(i == 1)
+        def _():
+            relay_raw(1, 0)
+
+        @pl.when(i == 3)
+        def _():
+            relay_raw(0, 0)
+            relay_raw(0, 2)
+
+    relay_raw(1, 3)
+
+    nrm[pl.ds(me, 1)] = sum(sq[:, k:k + 128] for k in range(0, half, 128))[None]
     for device in group:
         remote(nrm.at[me], nrm.at[me], nrm_send, nrm_recv, device)
     await_bytes(nrm.at[pl.ds(0, 7)], nrm_recv)
     total = jnp.sum(jnp.sum(nrm[...], axis=0), keepdims=True)
     factor = jnp.minimum(jnp.float32(1.0), bound / jnp.sqrt(total + 1e-06))
     fac[0] = jnp.broadcast_to(factor, fac.shape[1:])
-    for slot, device in ((1, z_up), (2, z_down), (3, y_up), (4, y_down)):
+    for slot, device in ((1, z_up), (2, z_down), (3, z_far), (4, y_up), (5, y_down), (6, y_far)):
         remote(fac.at[0], fac.at[slot], fac_send, fac_recv, device)
-    await_bytes(fac.at[pl.ds(1, 4)], fac_recv)
+    await_bytes(fac.at[pl.ds(1, 6)], fac_recv)
     scale = fac[0, 0:1, 0:1]
-    before = (fac[1, 0:1, 0:1], fac[3, 0:1, 0:1])
-    after = (fac[2, 0:1, 0:1], fac[4, 0:1, 0:1])
+    before, after, far = ([fac[k + 3 * h, 0:1, 0:1] for h in range(2)] for k in (1, 2, 3))
 
     def strips(size, body):
         @pl.loop(0, size // 16)
         def _(n):
             body(pl.multiple_of(n * 16, 16))
 
-    def away_of(i):
-        return jnp.where(i == 0, 2, jnp.where(i == 1, 1, jnp.where(i == 2, 3, 0)))
-
-    @pl.loop(0, RING)
-    def _(i):
-        for h in range(2):
-            v = turn(r[h], away_of(i))
-            await_bytes(r1.at[h, v], r1_recv.at[h, v])
-
-            def upper(n):
-                at = chunk(h, turn(q[h], 1), v, n, 16)
-                g[at, cols[h]] = (scale * g[at, cols[h]].astype(F32)
-                                  + before[h] * r1[h, v, pl.ds(n, 16)].astype(F32)).astype(BF16)
-
-            strips(up, upper)
-            remote(g.at[chunk(h, turn(q[h], 1), v, 0, up), cols[h]], fw.at[h, v, pl.ds(0, up)],
-                   fw_send.at[h, v], fw_recv.at[h, v], q_up[h])
-
-            def lower(n):
-                at = chunk(h, turn(q[h], -1), v, up + n, 16)
-                g[at, cols[h]] = (scale * g[at, cols[h]].astype(F32)
-                                  + after[h] * r1[h, v, pl.ds(up + n, 16)].astype(F32)).astype(BF16)
-
-            strips(down, lower)
-            remote(g.at[chunk(h, turn(q[h], -1), v, up, down), cols[h]], fw.at[h, v, pl.ds(up, down)],
-                   fw_send.at[h, v], fw_recv.at[h, v], q_down[h])
-
-    @pl.loop(0, RING)
-    def _(i):
-        away = away_of(i)
-        for h in range(2):
-            v = turn(r[h], away)
-            await_bytes(r2.at[h, v], r2_recv.at[h, v])
-            await_bytes(fw.at[h, v], fw_recv.at[h, v])
-
-            def gathered(other, start):
-                def body(n):
-                    n = start + n
-                    at = chunk(h, q[h], v, n, 16)
-                    g[at, cols[h]] = (scale * g[at, cols[h]].astype(F32)
-                                      + fw[h, v, pl.ds(n, 16)].astype(F32)
-                                      + other * r2[h, v, pl.ds(n, 16)].astype(F32)).astype(BF16)
-                return body
-
-            strips(up, gathered(after[h], 0))
-            strips(down, gathered(before[h], up))
-            upper = g.at[chunk(h, q[h], v, 0, up), cols[h]]
-            lower = g.at[chunk(h, q[h], v, up, down), cols[h]]
-
-            @pl.when(away == 1)
-            def _():
-                remote(lower, p2.at[h, pl.ds(up, down)], p_send.at[h], p2_recv.at[h], r_up[h])
-
-            @pl.when(away == 2)
-            def _():
-                remote(upper, p1.at[h, pl.ds(0, up)], p_send.at[h], p1_recv.at[h], r_up[h])
-                remote(lower, p1.at[h, pl.ds(up, down)], p_send.at[h], p1_recv.at[h], r_down[h])
-
-            @pl.when(away == 3)
-            def _():
-                remote(upper, p2.at[h, pl.ds(0, up)], p_send.at[h], p2_recv.at[h], r_down[h])
-
+    def pass_on(h, rel):
+        v = second(h, rel)
+        up = cuts[rel // 2]
+        await_bytes(r1.at[h, v], r1_recv.at[h, v])
+
+        def upper(n):
+            at = chunk(h, turn(q[h], 1), v, n, 16)
+            g[at, cols[h]] = (scale * g[at, cols[h]].astype(F32)
+                              + before[h] * r1[h, v, pl.ds(n, 16)].astype(F32)).astype(BF16)
+
+        strips(up, upper)
+        remote(g.at[chunk(h, turn(q[h], 1), v, 0, up), cols[h]], fw.at[h, v, pl.ds(0, up)],
+               fw_send.at[h, v], fw_recv.at[h, v], q_up[h])
+
+        def lower(n):
+            at = chunk(h, turn(q[h], -1), v, up + n, 16)
+            g[at, cols[h]] = (scale * g[at, cols[h]].astype(F32)
+                              + after[h] * r1[h, v, pl.ds(up + n, 16)].astype(F32)).astype(BF16)
+
+        strips(piece - up, lower)
+        remote(g.at[chunk(h, turn(q[h], -1), v, up, piece - up), cols[h]], fw.at[h, v, pl.ds(up, piece - up)],
+               fw_send.at[h, v], fw_recv.at[h, v], q_down[h])
+
+    upper_p, lower_p = pl.ds(0, cuts[0]), pl.ds(cuts[0], piece - cuts[0])
+
+    def send_second(h, v):
+        away = turn(v - r[h], 0)
+        upper = g.at[chunk(h, q[h], v, 0, cuts[0]), cols[h]]
+        lower = g.at[chunk(h, q[h], v, cuts[0], piece - cuts[0]), cols[h]]
+
+        @pl.when(away == 1)
+        def _():
+            remote(lower, p2.at[h, lower_p], p_send.at[h], p2_recv.at[h], r_up[h])
+
+        @pl.when(away == 2)
+        def _():
+            remote(upper, p1.at[h, upper_p], p_send.at[h], p1_recv.at[h], r_up[h])
+            remote(lower, p1.at[h, lower_p], p_send.at[h], p1_recv.at[h], r_down[h])
+
+        @pl.when(away == 3)
+        def _():
+            remote(upper, p2.at[h, upper_p], p_send.at[h], p2_recv.at[h], r_down[h])
+
+    def gather_direct(h, rel):
+        v = second(h, rel)
+        await_bytes(g.at[pl.ds(0, 2 * piece), cols[h]], r2_recv.at[h, v])
+        await_bytes(fw.at[h, v], fw_recv.at[h, v])
+
+        def body(n):
+            at, part = chunk(h, q[h], v, n, 16), pl.ds(n, 16)
+            g[at, cols[h]] = (scale * g[at, cols[h]].astype(F32) + far[h] * fw[h, v, part].astype(F32)
+                              + before[h] * from_down[h, v, part].astype(F32)
+                              + after[h] * from_up[h, v, part].astype(F32)).astype(BF16)
+
+        strips(piece, body)
+        send_second(h, v)
+
+    def gather_passed(h, rel):
+        v = second(h, rel)
+        up = cuts[rel // 2]
+        await_bytes(g.at[pl.ds(0, piece), cols[h]], r2_recv.at[h, v])
+        await_bytes(fw.at[h, v], fw_recv.at[h, v])
+
+        def gathered(other, ref, start):
+            def body(n):
+                n = start + n
+                at, part = chunk(h, q[h], v, n, 16), pl.ds(n, 16)
+                g[at, cols[h]] = (scale * g[at, cols[h]].astype(F32) + fw[h, v, part].astype(F32)
+                                  + other * ref[h, v, part].astype(F32)).astype(BF16)
+            return body
+
+        strips(up, gathered(after[h], from_up, 0))
+        strips(piece - up, gathered(before[h], from_down, up))
+        send_second(h, v)
+
+    for h, rel in ((1, 1), (0, 1), (0, 3), (1, 2)):
+        pass_on(h, rel)
+    for h, rel in ((0, 0), (1, 0), (0, 2), (1, 3)):
+        gather_direct(h, rel)
+    for h, rel in ((1, 1), (0, 1), (0, 3), (1, 2)):
+        gather_passed(h, rel)
+
+    up, down = cuts[0], piece - cuts[0]
     for h in range(2):
         await_bytes(p1.at[h], p1_recv.at[h])
 
@@ -300,13 +353,14 @@
 
     def relay(h, away):
         v = turn(r[h], away)
+        up = cuts[away % 2]
         u = turn(q[h], -1)
         await_bytes(place(h, u, v), ag2_recv.at[h, v, 0])
         at = place(h, u, v, 0, up)
         remote(at, at, ag2_send.at[h, away], ag2_recv.at[h, v, 2], q_up[h])
         u = turn(q[h], 1)
         await_bytes(place(h, u, v), ag2_recv.at[h, v, 1])
-        at = place(h, u, v, up, down)
+        at = place(h, u, v, up, piece - up)
         remote(at, at, ag2_send.at[h, away], ag2_recv.at[h, v, 2], q_down[h])
 
     for h in range(2):
@@ -326,15 +380,17 @@
     for h in range(2):
         await_bytes(g.at[pl.ds(0, 3 * piece), cols[0]], p_send.at[h])
         await_bytes(g.at[pl.ds(0, 3 * piece), cols[0]], ag1_send.at[h])
+        for rel in range(RING):
+            rows_out = (3 if (rel % 2 == 0 if h == 0 else rel in (0, 3)) else 2) * piece
+            await_bytes(g.at[pl.ds(0, rows_out), cols[0]], raw_send.at[h, second(h, rel)])
         for b in range(RING):
-            await_bytes(g.at[pl.ds(0, 2 * piece), cols[0]], raw_send.at[h, b])
             await_bytes(g.at[pl.ds(0, piece), cols[0]], fw_send.at[h, b])
             await_bytes(g.at[pl.ds(0, 3 * piece), cols[0]], ag2_send.at[h, b])
     for side in range(2):
         for m in (4, 5):
             await_bytes(ot_v.at[pl.ds(0, piece)], x_send.at[side, m])
     await_bytes(nrm.at[pl.ds(0, 7)], nrm_send)
-    await_bytes(fac.at[pl.ds(1, 4)], fac_send)
+    await_bytes(fac.at[pl.ds(1, 6)], fac_send)
 
 
 def on_device(hidden, out_grad, lengths, noise):
@@ -357,13 +413,14 @@
             pltpu.VMEM((2, RING, piece, half), BF16),
             pltpu.VMEM((2, RING, piece, half), BF16),
             pltpu.VMEM((2, RING, piece, half), BF16),
+            pltpu.VMEM((2, RING, piece, half), BF16),
             pltpu.VMEM((2, piece, half), BF16),
             pltpu.VMEM((2, piece, half), BF16),
             pltpu.VMEM((2, piece, half), BF16),
             pltpu.VMEM((piece, units), F32),
-            pltpu.VMEM((8, 256), F32),
+            pltpu.VMEM((8, half), F32),
             pltpu.VMEM((2 * RING, 8, 128), F32),
-            pltpu.VMEM((5, 8, 128), F32),
+            pltpu.VMEM((7, 8, 128), F32),
             dma((3,)), dma((2, 6)), dma((2, 6)),
             dma((2, RING)), dma((2, RING)), dma((2, RING)), dma((2, RING)), dma((2, RING)),
             dma((2,)), dma((2,)), dma((2,)), dma((2,)),
@@ -371,7 +428,7 @@
             dma((2,)), dma((2, 3)), dma((2, RING)), dma((2, RING, 3)),
         ],
         compiler_params=pltpu.CompilerParams(
-            collective_id=0, has_side_effects=True, vmem_limit_bytes=40 * 1024 * 1024
+            collective_id=0, has_side_effects=True, vmem_limit_bytes=44 * 1024 * 1024
         ),
         cost_estimate=pl.CostEstimate(
             flops=2 * width * units * seq_len, bytes_accessed=30_000_000, transcendentals=0

time: 149 us -> 146 us (0.980)
  Pallas kernels: 144 us -> 141 us
    pallas_call x1, Pallas kernels: 144 us -> 141 us  [on_device(): pl.pallas_call(functools.partial(kernel, bound), out_shape=pltpu.VMEM((wi...]
where the time goes in v3:
time: 146 us
  Pallas kernels  141 us (97%)
  local copies, waits for them, and re-layouts  4.13 us (3%)
    pallas_call x1, Pallas kernels, on_device(): pl.pallas_call(functools.partial(kernel, bound), out_shape=pltpu.VMEM((wi...  141 us
    unnamed x1, local copies, waits for them, and re-layouts  4.13 us

profile of v3, /device:TPU:0, one launch (start us, length us, event | category | flops | bytes accessed | tf_op | source)
XLA Modules:
  0.0 146.2 jit_solution(8182697741816346327)
XLA Ops:
  0.7 141.4 %shard_map.46 = bf16[2304,2304]{1,0:T(8,128)(2,1)S(1)} custom-call(s32[1]{0:T(128)S(6)} %copy.7.len_ref, bf16[576,1024]{1,0:T(8,128)(2,1)} %bitcast.9, bf16[1024,2304]{1,0:T(8,128)(2,1)} %bitcast.7, f32[144,2304]{1,0:T(8,128)} %bitcast.8), custom_call_target="tpu_custom_call" | custom-call | flops 10871635968 | bytes 30000000 | tf_op jit(solution)/shard_map/pallas_call | solution.py:404
  142.1 4.1 %copy.6 = bf16[1,2304,2304]{2,1,0:T(8,128)(2,1)} copy(bf16[1,2304,2304]{2,1,0:T(8,128)(2,1)S(1)} %bitcast.6) | data formatting | bytes 21233664

commit v4 on v3

--- a/solution.py
+++ b/solution.py
@@ -10,13 +10,14 @@
 MESH = pl.DeviceIdType.MESH
 RING = 4
 F32 = jnp.float32
+DIRECT = ((0,), (0,))
 BF16 = jnp.bfloat16
 
 
 def kernel(bound, len_ref, o_hbm, h_hbm, noise_hbm, out,
-           h_v, ot_v, g, r1, from_down, from_up, fw, p1, p2, pf, nz, sq, nrm, fac,
+           h_v, ot_v, g, r1, from_down, from_up, fw, p1, p2, pf, nz, nz_low, nz_mid, sq, nrm, fac,
            load_sem, x_send, x_recv, raw_send, r1_recv, r2_recv, fw_send, fw_recv,
-           p_send, p1_recv, p2_recv, pf_recv, nrm_send, nrm_recv,
+           p_send, p1_recv, p2_recv, pf_recv, nz_send, nz_recv, mid_send, mid_recv, nrm_send, nrm_recv,
            fac_send, fac_recv, ag1_send, ag1_recv, ag2_send, ag2_recv):
     dp = lax.axis_index("dp")
     x = lax.axis_index("tensor")
@@ -43,8 +44,8 @@
     def rows(b, p, start=0, size=None):
         return pl.ds(pl.multiple_of(b * block + p * piece + start, 16), piece if size is None else size)
 
-    def chunk(h, u, v, start=0, size=None):
-        return rows(u, v, start, size) if h == 0 else rows(v, u, start, size)
+    def chunk(u, v, start=0, size=None):
+        return rows(v, u, start, size)
 
     def remote(src, dst, send, recv, device):
         pltpu.make_async_remote_copy(src_ref=src, dst_ref=dst, send_sem=send, recv_sem=recv,
@@ -71,13 +72,11 @@
     for device in group + [z_up, z_down, z_far, y_up, y_down, y_far]:
         pl.semaphore_signal(barrier, inc=1, device_id=device, device_id_type=MESH)
 
-    pl.semaphore_wait(barrier, 13)
-
     def passed_on(m):
-        return (m == 2) | (m == 5)
+        return m >= RING
 
     def first(m):
-        return jnp.where((m == 0) | (m == 2), 0, jnp.where(m == 1, 2, jnp.where(m == 4, 3, 1)))
+        return jnp.where((m == 0) | (m == 4), 0, jnp.where(m == 1, 2, jnp.where(m == 3, 3, 1)))
 
     def x_start_up(m):
         at = ot_v.at[rows(jnp.where(passed_on(m), turn(x, -1), x), first(m))]
@@ -89,30 +88,50 @@
 
     load_o.wait()
     kept = lax.broadcasted_iota(jnp.int32, (16, tokens), 1) < len_ref[0]
-    for p in (0, 2, 1, 3):
-        @pl.loop(0, piece // 16)
-        def _(n):
-            at = rows(x, p, n * 16, 16)
-            ot_v[at] = jnp.where(kept, ot_v[at], jnp.zeros((), BF16))
-
-        if p == 2:
-            for m in range(2):
-                x_start_up(jnp.int32(m))
-                x_start_down(jnp.int32(m))
+
+    @pl.loop(0, block // 16)
+    def _(n):
+        at = rows(x, 0, n * 16, 16)
+        ot_v[at] = jnp.where(kept, ot_v[at], jnp.zeros((), BF16))
 
     sq[...] = jnp.zeros_like(sq)
+    pl.semaphore_wait(barrier, 13)
+    for m in range(2):
+        x_start_up(jnp.int32(m))
+        x_start_down(jnp.int32(m))
+
+    load_n.wait()
+
+    @pl.loop(0, piece // 16)
+    def _(n):
+        at = pl.ds(pl.multiple_of(n * 16, 16), 16)
+        low = nz[at, cols[0]].astype(BF16)
+        nz_low[0, at] = low
+
+        @pl.when(z == y)
+        def _():
+            nz_low[1, at] = low
+
+    above, below = pl.ds(0, cuts[0]), pl.ds(cuts[0], piece - cuts[0])
+
+    @pl.when(z != y)
+    def _():
+        remote(nz_low.at[0, above], nz_mid.at[z, above], nz_send, mid_recv, {"dp": y * RING + y})
+        remote(nz_low.at[0, below], nz_mid.at[y, below], nz_send, mid_recv, {"dp": z * RING + z})
+
     load_h.wait()
 
-    def kind(h, b, p):
-        if h == 0:
-            return p // 2, p % 2 == 0
+    def kind(h, b):
         ahead = turn(b - x, 0)
-        return ahead // 2, (ahead == 0) | (ahead == 3)
-
-    def send_raw(h, b, p):
-        u, v = (b, p) if h == 0 else (p, b)
+        direct = ahead == DIRECT[h][0]
+        for rel in DIRECT[h][1:]:
+            direct = direct | (ahead == rel)
+        return ahead // 2, direct
+
+    def send_raw(h, v, u):
+        b, p = v, u
         away = turn(u - q[h], 0)
-        cut, direct = kind(h, b, p)
+        cut, direct = kind(h, b)
         whole = g.at[rows(b, p), cols[h]]
 
         @pl.when(direct & (away == 1))
@@ -152,7 +171,7 @@
             send_raw(h, bb, pb)
 
     def second(h, rel):
-        return rel if h == 0 else turn(x, rel)
+        return turn(x, rel)
 
     def relay_raw(h, rel):
         v = second(h, rel)
@@ -166,6 +185,14 @@
     def _(i):
         product(x, 2 * i, x, 2 * i + 1)
 
+    @pl.when(z == y)
+    def _():
+        await_bytes(nz_mid.at[pl.ds(0, 3)], mid_recv)
+        for k in range(1, RING):
+            other = turn(z, k)
+            remote(nz_mid.at[other, above], nz_low.at[1, above], mid_send, nz_recv, {"dp": z * RING + other})
+            remote(nz_mid.at[other, below], nz_low.at[1, below], mid_send, nz_recv, {"dp": other * RING + z})
+
     @pl.loop(0, 6)
     def _(i):
         ba, pa = jnp.where(passed_on(i), turn(x, 2), turn(x, -1)), first(i)
@@ -184,14 +211,14 @@
 
         @pl.when(i == 1)
         def _():
-            relay_raw(1, 0)
-
-        @pl.when(i == 3)
-        def _():
-            relay_raw(0, 0)
-            relay_raw(0, 2)
-
-    relay_raw(1, 3)
+            for h in range(2):
+                relay_raw(h, 0)
+
+        @pl.when(i == 4)
+        def _():
+            for h in range(2):
+                for rel in DIRECT[h][1:]:
+                    relay_raw(h, rel)
 
     nrm[pl.ds(me, 1)] = sum(sq[:, k:k + 128] for k in range(0, half, 128))[None]
     for device in group:
@@ -211,35 +238,36 @@
         def _(n):
             body(pl.multiple_of(n * 16, 16))
 
-    def pass_on(h, rel):
-        v = second(h, rel)
-        up = cuts[rel // 2]
+    def away_of(i):
+        return jnp.where(i == 0, 2, jnp.where(i == 1, 1, jnp.where(i == 2, 3, 0)))
+
+    def pass_on(h, v, up):
         await_bytes(r1.at[h, v], r1_recv.at[h, v])
 
         def upper(n):
-            at = chunk(h, turn(q[h], 1), v, n, 16)
+            at = chunk(turn(q[h], 1), v, n, 16)
             g[at, cols[h]] = (scale * g[at, cols[h]].astype(F32)
                               + before[h] * r1[h, v, pl.ds(n, 16)].astype(F32)).astype(BF16)
 
         strips(up, upper)
-        remote(g.at[chunk(h, turn(q[h], 1), v, 0, up), cols[h]], fw.at[h, v, pl.ds(0, up)],
+        remote(g.at[chunk(turn(q[h], 1), v, 0, up), cols[h]], fw.at[h, v, pl.ds(0, up)],
                fw_send.at[h, v], fw_recv.at[h, v], q_up[h])
 
         def lower(n):
-            at = chunk(h, turn(q[h], -1), v, up + n, 16)
+            at = chunk(turn(q[h], -1), v, up + n, 16)
             g[at, cols[h]] = (scale * g[at, cols[h]].astype(F32)
                               + after[h] * r1[h, v, pl.ds(up + n, 16)].astype(F32)).astype(BF16)
 
         strips(piece - up, lower)
-        remote(g.at[chunk(h, turn(q[h], -1), v, up, piece - up), cols[h]], fw.at[h, v, pl.ds(up, piece - up)],
+        remote(g.at[chunk(turn(q[h], -1), v, up, piece - up), cols[h]], fw.at[h, v, pl.ds(up, piece - up)],
                fw_send.at[h, v], fw_recv.at[h, v], q_down[h])
 
     upper_p, lower_p = pl.ds(0, cuts[0]), pl.ds(cuts[0], piece - cuts[0])
 
     def send_second(h, v):
         away = turn(v - r[h], 0)
-        upper = g.at[chunk(h, q[h], v, 0, cuts[0]), cols[h]]
-        lower = g.at[chunk(h, q[h], v, cuts[0], piece - cuts[0]), cols[h]]
+        upper = g.at[chunk(q[h], v, 0, cuts[0]), cols[h]]
+        lower = g.at[chunk(q[h], v, cuts[0], piece - cuts[0]), cols[h]]
 
         @pl.when(away == 1)
         def _():
@@ -254,13 +282,12 @@
         def _():
             remote(upper, p2.at[h, upper_p], p_send.at[h], p2_recv.at[h], r_down[h])
 
-    def gather_direct(h, rel):
-        v = second(h, rel)
+    def gather_direct(h, v):
         await_bytes(g.at[pl.ds(0, 2 * piece), cols[h]], r2_recv.at[h, v])
         await_bytes(fw.at[h, v], fw_recv.at[h, v])
 
         def body(n):
-            at, part = chunk(h, q[h], v, n, 16), pl.ds(n, 16)
+            at, part = chunk(q[h], v, n, 16), pl.ds(n, 16)
             g[at, cols[h]] = (scale * g[at, cols[h]].astype(F32) + far[h] * fw[h, v, part].astype(F32)
                               + before[h] * from_down[h, v, part].astype(F32)
                               + after[h] * from_up[h, v, part].astype(F32)).astype(BF16)
@@ -268,16 +295,14 @@
         strips(piece, body)
         send_second(h, v)
 
-    def gather_passed(h, rel):
-        v = second(h, rel)
-        up = cuts[rel // 2]
+    def gather_passed(h, v, up):
         await_bytes(g.at[pl.ds(0, piece), cols[h]], r2_recv.at[h, v])
         await_bytes(fw.at[h, v], fw_recv.at[h, v])
 
         def gathered(other, ref, start):
             def body(n):
                 n = start + n
-                at, part = chunk(h, q[h], v, n, 16), pl.ds(n, 16)
+                at, part = chunk(q[h], v, n, 16), pl.ds(n, 16)
                 g[at, cols[h]] = (scale * g[at, cols[h]].astype(F32) + fw[h, v, part].astype(F32)
                                   + other * ref[h, v, part].astype(F32)).astype(BF16)
             return body
@@ -286,35 +311,59 @@
         strips(piece - up, gathered(before[h], from_down, up))
         send_second(h, v)
 
-    for h, rel in ((1, 1), (0, 1), (0, 3), (1, 2)):
-        pass_on(h, rel)
-    for h, rel in ((0, 0), (1, 0), (0, 2), (1, 3)):
-        gather_direct(h, rel)
-    for h, rel in ((1, 1), (0, 1), (0, 3), (1, 2)):
-        gather_passed(h, rel)
-
     up, down = cuts[0], piece - cuts[0]
-    for h in range(2):
+
+    def pass_second(h):
         await_bytes(p1.at[h], p1_recv.at[h])
 
         def upper(n):
-            at = chunk(h, q[h], turn(r[h], 1), n, 16)
+            at = chunk(q[h], turn(r[h], 1), n, 16)
             g[at, cols[h]] = (g[at, cols[h]].astype(F32) + p1[h, pl.ds(n, 16)].astype(F32)).astype(BF16)
 
         strips(up, upper)
-        remote(g.at[chunk(h, q[h], turn(r[h], 1), 0, up), cols[h]], pf.at[h, pl.ds(0, up)],
+        remote(g.at[chunk(q[h], turn(r[h], 1), 0, up), cols[h]], pf.at[h, pl.ds(0, up)],
                p_send.at[h], pf_recv.at[h], r_up[h])
 
         def lower(n):
-            at = chunk(h, q[h], turn(r[h], -1), up + n, 16)
+            at = chunk(q[h], turn(r[h], -1), up + n, 16)
             g[at, cols[h]] = (g[at, cols[h]].astype(F32) + p1[h, pl.ds(up + n, 16)].astype(F32)).astype(BF16)
 
         strips(down, lower)
-        remote(g.at[chunk(h, q[h], turn(r[h], -1), up, down), cols[h]], pf.at[h, pl.ds(up, down)],
+        remote(g.at[chunk(q[h], turn(r[h], -1), up, down), cols[h]], pf.at[h, pl.ds(up, down)],
                p_send.at[h], pf_recv.at[h], r_down[h])
 
+    @pl.loop(0, RING)
+    def _(i):
+        for h in range(2):
+            v = turn(r[h], away_of(i))
+            cut, direct = kind(h, v)
+            for k in range(2):
+                @pl.when((cut == k) & ~direct)
+                def _():
+                    pass_on(h, v, cuts[k])
+
+    @pl.loop(0, RING)
+    def _(i):
+        @pl.when(i == RING - 1)
+        def _():
+            for h in range(2):
+                pass_second(h)
+
+        for h in range(2):
+            v = turn(r[h], away_of(i))
+            cut, direct = kind(h, v)
+
+            @pl.when(direct)
+            def _():
+                gather_direct(h, v)
+
+            for k in range(2):
+                @pl.when((cut == k) & ~direct)
+                def _():
+                    gather_passed(h, v, cuts[k])
+
     def place(h, u, v, start=0, size=None):
-        return out.at[chunk(h, u, v, start, size), cols[h]]
+        return out.at[chunk(u, v, start, size), cols[h]]
 
     def spread(h, away):
         v = turn(r[h], away)
@@ -322,16 +371,19 @@
         remote(at, at, ag2_send.at[h, away], ag2_recv.at[h, v, 0], q_up[h])
         remote(at, at, ag2_send.at[h, away], ag2_recv.at[h, v, 1], q_down[h])
 
-    load_n.wait()
+    @pl.when(z != y)
+    def _():
+        await_bytes(nz_low.at[1], nz_recv)
+
     for h in range(2):
         await_bytes(p2.at[h], p2_recv.at[h])
         await_bytes(pf.at[h], pf_recv.at[h])
 
         def final(n):
             at = pl.ds(n, 16)
-            whole = (g[chunk(h, q[h], r[h], n, 16), cols[h]].astype(F32) + p2[h, at].astype(F32)
-                     + pf[h, at].astype(F32) + nz[at, cols[h]])
-            out[chunk(h, q[h], r[h], n, 16), cols[h]] = (whole * (1.0 / 16.0)).astype(BF16)
+            whole = (g[chunk(q[h], r[h], n, 16), cols[h]].astype(F32) + p2[h, at].astype(F32)
+                     + pf[h, at].astype(F32) + (nz_low[1, at].astype(F32) if h == 0 else nz[at, cols[1]]))
+            out[chunk(q[h], r[h], n, 16), cols[h]] = (whole * (1.0 / 16.0)).astype(BF16)
 
         strips(piece, final)
         mine = place(h, q[h], r[h])
@@ -381,7 +433,7 @@
         await_bytes(g.at[pl.ds(0, 3 * piece), cols[0]], p_send.at[h])
         await_bytes(g.at[pl.ds(0, 3 * piece), cols[0]], ag1_send.at[h])
         for rel in range(RING):
-            rows_out = (3 if (rel % 2 == 0 if h == 0 else rel in (0, 3)) else 2) * piece
+            rows_out = (3 if rel in DIRECT[h] else 2) * piece
             await_bytes(g.at[pl.ds(0, rows_out), cols[0]], raw_send.at[h, second(h, rel)])
         for b in range(RING):
             await_bytes(g.at[pl.ds(0, piece), cols[0]], fw_send.at[h, b])
@@ -389,6 +441,14 @@
     for side in range(2):
         for m in (4, 5):
             await_bytes(ot_v.at[pl.ds(0, piece)], x_send.at[side, m])
+    @pl.when(z != y)
+    def _():
+        await_bytes(nz_low.at[0], nz_send)
+
+    @pl.when(z == y)
+    def _():
+        await_bytes(nz_mid.at[pl.ds(0, 3)], mid_send)
+
     await_bytes(nrm.at[pl.ds(0, 7)], nrm_send)
     await_bytes(fac.at[pl.ds(1, 6)], fac_send)
 
@@ -418,17 +478,19 @@
             pltpu.VMEM((2, piece, half), BF16),
             pltpu.VMEM((2, piece, half), BF16),
             pltpu.VMEM((piece, units), F32),
+            pltpu.VMEM((2, piece, half), BF16),
+            pltpu.VMEM((RING, piece, half), BF16),
             pltpu.VMEM((8, half), F32),
             pltpu.VMEM((2 * RING, 8, 128), F32),
             pltpu.VMEM((7, 8, 128), F32),
             dma((3,)), dma((2, 6)), dma((2, 6)),
             dma((2, RING)), dma((2, RING)), dma((2, RING)), dma((2, RING)), dma((2, RING)),
             dma((2,)), dma((2,)), dma((2,)), dma((2,)),
-            dma, dma, dma, dma,
+            dma, dma, dma, dma, dma, dma, dma, dma,
             dma((2,)), dma((2, 3)), dma((2, RING)), dma((2, RING, 3)),
         ],
         compiler_params=pltpu.CompilerParams(
-            collective_id=0, has_side_effects=True, vmem_limit_bytes=44 * 1024 * 1024
+            collective_id=0, has_side_effects=True, vmem_limit_bytes=46 * 1024 * 1024
         ),
         cost_estimate=pl.CostEstimate(
             flops=2 * width * units * seq_len, bytes_accessed=30_000_000, transcendentals=0

time: 146 us -> 141 us (0.966)
  Pallas kernels: 141 us -> 136 us
    pallas_call x1, Pallas kernels: 141 us -> 136 us  [on_device(): pl.pallas_call(functools.partial(kernel, bound), out_shape=pltpu.VMEM((wi...]
where the time goes in v4:
time: 141 us
  Pallas kernels  136 us (96%)
  local copies, waits for them, and re-layouts  4.13 us (3%)
    pallas_call x1, Pallas kernels, on_device(): pl.pallas_call(functools.partial(kernel, bound), out_shape=pltpu.VMEM((wi...  136 us
    unnamed x1, local copies, waits for them, and re-layouts  4.13 us

profile of v4, /device:TPU:0, one launch (start us, length us, event | category | flops | bytes accessed | tf_op | source)
XLA Modules:
  0.0 140.7 jit_solution(12142915099882470055)
XLA Ops:
  0.7 135.9 %shard_map.46 = bf16[2304,2304]{1,0:T(8,128)(2,1)S(1)} custom-call(s32[1]{0:T(128)S(6)} %copy.7.len_ref, bf16[576,1024]{1,0:T(8,128)(2,1)} %bitcast.9, bf16[1024,2304]{1,0:T(8,128)(2,1)} %bitcast.7, f32[144,2304]{1,0:T(8,128)} %bitcast.8), custom_call_target="tpu_custom_call" | custom-call | flops 10871635968 | bytes 30000000 | tf_op jit(solution)/shard_map/pallas_call | solution.py:464
  136.6 4.1 %copy.6 = bf16[1,2304,2304]{2,1,0:T(8,128)(2,1)} copy(bf16[1,2304,2304]{2,1,0:T(8,128)(2,1)S(1)} %bitcast.6) | data formatting | bytes 21233664

commit v5 on v4

--- a/solution.py
+++ b/solution.py
@@ -18,7 +18,7 @@
            h_v, ot_v, g, r1, from_down, from_up, fw, p1, p2, pf, nz, nz_low, nz_mid, sq, nrm, fac,
            load_sem, x_send, x_recv, raw_send, r1_recv, r2_recv, fw_send, fw_recv,
            p_send, p1_recv, p2_recv, pf_recv, nz_send, nz_recv, mid_send, mid_recv, nrm_send, nrm_recv,
-           fac_send, fac_recv, ag1_send, ag1_recv, ag2_send, ag2_recv):
+           fac_send, fac_recv, far_recv, ag1_send, ag1_recv, ag2_send, ag2_recv):
     dp = lax.axis_index("dp")
     x = lax.axis_index("tensor")
     core = lax.axis_index("layer")
@@ -78,27 +78,21 @@
     def first(m):
         return jnp.where((m == 0) | (m == 4), 0, jnp.where(m == 1, 2, jnp.where(m == 3, 3, 1)))
 
-    def x_start_up(m):
-        at = ot_v.at[rows(jnp.where(passed_on(m), turn(x, -1), x), first(m))]
-        remote(at, at, x_send.at[0, m], x_recv.at[0, m], x_up)
-
-    def x_start_down(m):
-        at = ot_v.at[rows(jnp.where(passed_on(m), turn(x, 1), x), (first(m) + 2) % RING)]
-        remote(at, at, x_send.at[1, m], x_recv.at[1, m], x_down)
-
-    load_o.wait()
-    kept = lax.broadcasted_iota(jnp.int32, (16, tokens), 1) < len_ref[0]
-
-    @pl.loop(0, block // 16)
-    def _(n):
-        at = rows(x, 0, n * 16, 16)
-        ot_v[at] = jnp.where(kept, ot_v[at], jnp.zeros((), BF16))
+    def x_start(side, m, own, start=0, size=None):
+        p = (first(m) + 2 * side) % RING
+        device = (x_up, x_down)[side]
+        if own:
+            remote(o_hbm.at[pl.ds(pl.multiple_of(p * piece, 16), piece)], ot_v.at[rows(x, p)],
+                   x_send.at[side, m], x_recv.at[side, m], device)
+        else:
+            at = ot_v.at[rows(turn(x, 2 * side - 1), p, start, size)]
+            remote(at, at, x_send.at[side, m], x_recv.at[side, m], device)
 
     sq[...] = jnp.zeros_like(sq)
     pl.semaphore_wait(barrier, 13)
-    for m in range(2):
-        x_start_up(jnp.int32(m))
-        x_start_down(jnp.int32(m))
+    for side in range(2):
+        for m in range(2):
+            x_start(side, jnp.int32(m), True)
 
     load_n.wait()
 
@@ -120,6 +114,13 @@
         remote(nz_low.at[0, below], nz_mid.at[y, below], nz_send, mid_recv, {"dp": z * RING + z})
 
     load_h.wait()
+    load_o.wait()
+
+    @pl.loop(0, tokens // 16)
+    def _(n):
+        at = pl.ds(pl.multiple_of(n * 16, 16), 16)
+        kept = n * 16 + lax.broadcasted_iota(jnp.int32, (16, units), 0) < len_ref[0]
+        h_v[at] = jnp.where(kept, h_v[at], jnp.zeros((), BF16))
 
     def kind(h, b):
         ahead = turn(b - x, 0)
@@ -159,16 +160,20 @@
                 remote(upper, r1.at[h, v, above], raw_send.at[h, v], r1_recv.at[h, v], q_up[h])
                 remote(lower, r1.at[h, v, below], raw_send.at[h, v], r1_recv.at[h, v], q_down[h])
 
-    def product(ba, pa, bb, pb):
+    def product(ba, pa, bb, pb, start=0, size=piece):
+        ra, rb = rows(ba, pa, start, size), rows(bb, pb, start, size)
         for h in range(2):
-            left = jnp.concatenate([ot_v[rows(ba, pa)], ot_v[rows(bb, pb)]], axis=0)
+            left = jnp.concatenate([ot_v[ra], ot_v[rb]], axis=0)
             result = jnp.dot(left, h_v[:, cols[h]], preferred_element_type=F32)
-            sq[...] += jnp.sum((result * result).reshape(2 * piece // 8, 8, half), axis=0)
+            sq[...] += jnp.sum((result * result).reshape(2 * size // 8, 8, half), axis=0)
             low = result.astype(BF16)
-            g[rows(ba, pa), cols[h]] = low[:piece]
-            g[rows(bb, pb), cols[h]] = low[piece:]
-            send_raw(h, ba, pa)
-            send_raw(h, bb, pb)
+            g[ra, cols[h]] = low[:size]
+            g[rb, cols[h]] = low[size:]
+
+    def send_all(*pieces):
+        for b, p in pieces:
+            for h in range(2):
+                send_raw(h, b, p)
 
     def second(h, rel):
         return turn(x, rel)
@@ -184,16 +189,9 @@
     @pl.loop(0, 2)
     def _(i):
         product(x, 2 * i, x, 2 * i + 1)
-
-    @pl.when(z == y)
-    def _():
-        await_bytes(nz_mid.at[pl.ds(0, 3)], mid_recv)
-        for k in range(1, RING):
-            other = turn(z, k)
-            remote(nz_mid.at[other, above], nz_low.at[1, above], mid_send, nz_recv, {"dp": z * RING + other})
-            remote(nz_mid.at[other, below], nz_low.at[1, below], mid_send, nz_recv, {"dp": other * RING + z})
-
-    @pl.loop(0, 6)
+        send_all((x, 2 * i), (x, 2 * i + 1))
+
+    @pl.loop(0, 5)
     def _(i):
         ba, pa = jnp.where(passed_on(i), turn(x, 2), turn(x, -1)), first(i)
         bb, pb = jnp.where(passed_on(i), turn(x, 2), turn(x, 1)), (first(i) + 2) % RING
@@ -204,34 +202,65 @@
         def _():
             await_bytes(ot_v.at[pl.ds(0, piece)], x_send.at[0, i])
             await_bytes(ot_v.at[pl.ds(0, piece)], x_send.at[1, i])
-            x_start_up(i + 2)
-            x_start_down(i + 2)
+
+        for side in range(2):
+            @pl.when(i + 2 < RING)
+            def _():
+                x_start(side, i + 2, True)
+
+            @pl.when(i == 2)
+            def _():
+                x_start(side, i + 2, False)
+
+            @pl.when(i == 3)
+            def _():
+                x_start(side, i + 2, False, 0, cuts[0])
+                x_start(side, i + 3, False, cuts[0], cuts[1])
 
         product(ba, pa, bb, pb)
+
+        send_all((ba, pa), (bb, pb))
+
+        @pl.when((z == y) & (i == 1))
+        def _():
+            await_bytes(nz_mid.at[pl.ds(0, 3)], mid_recv)
+            for k in range(1, RING):
+                other = turn(z, k)
+                remote(nz_mid.at[other, above], nz_low.at[1, above], mid_send, nz_recv, {"dp": z * RING + other})
+                remote(nz_mid.at[other, below], nz_low.at[1, below], mid_send, nz_recv, {"dp": other * RING + z})
+
 
         @pl.when(i == 1)
         def _():
             for h in range(2):
                 relay_raw(h, 0)
 
-        @pl.when(i == 4)
-        def _():
-            for h in range(2):
-                for rel in DIRECT[h][1:]:
-                    relay_raw(h, rel)
+    far_block = turn(x, 2)
+    for m, start, size in ((5, 0, cuts[0]), (6, cuts[0], cuts[1])):
+        for side, p in enumerate((1, 3)):
+            await_bytes(ot_v.at[rows(far_block, p, start, size)], x_recv.at[side, m])
+        product(far_block, 1, far_block, 3, start, size)
 
     nrm[pl.ds(me, 1)] = sum(sq[:, k:k + 128] for k in range(0, half, 128))[None]
     for device in group:
         remote(nrm.at[me], nrm.at[me], nrm_send, nrm_recv, device)
+    send_all((far_block, 1), (far_block, 3))
+
+    for h in range(2):
+        for rel in DIRECT[h][1:]:
+            relay_raw(h, rel)
+
     await_bytes(nrm.at[pl.ds(0, 7)], nrm_recv)
     total = jnp.sum(jnp.sum(nrm[...], axis=0), keepdims=True)
     factor = jnp.minimum(jnp.float32(1.0), bound / jnp.sqrt(total + 1e-06))
     fac[0] = jnp.broadcast_to(factor, fac.shape[1:])
-    for slot, device in ((1, z_up), (2, z_down), (3, z_far), (4, y_up), (5, y_down), (6, y_far)):
+    for slot, device in ((1, z_up), (2, z_down), (3, y_up), (4, y_down)):
         remote(fac.at[0], fac.at[slot], fac_send, fac_recv, device)
-    await_bytes(fac.at[pl.ds(1, 6)], fac_recv)
+    for slot, device in ((5, z_far), (6, y_far)):
+        remote(fac.at[0], fac.at[slot], fac_send, far_recv, device)
+    await_bytes(fac.at[pl.ds(1, 4)], fac_recv)
     scale = fac[0, 0:1, 0:1]
-    before, after, far = ([fac[k + 3 * h, 0:1, 0:1] for h in range(2)] for k in (1, 2, 3))
+    before, after = ([fac[k + 2 * h, 0:1, 0:1] for h in range(2)] for k in (1, 2))
 
     def strips(size, body):
         @pl.loop(0, size // 16)
@@ -341,6 +370,9 @@
                 @pl.when((cut == k) & ~direct)
                 def _():
                     pass_on(h, v, cuts[k])
+
+    await_bytes(fac.at[pl.ds(5, 2)], far_recv)
+    far = [fac[5 + h, 0:1, 0:1] for h in range(2)]
 
     @pl.loop(0, RING)
     def _(i):
@@ -439,8 +471,8 @@
             await_bytes(g.at[pl.ds(0, piece), cols[0]], fw_send.at[h, b])
             await_bytes(g.at[pl.ds(0, 3 * piece), cols[0]], ag2_send.at[h, b])
     for side in range(2):
-        for m in (4, 5):
-            await_bytes(ot_v.at[pl.ds(0, piece)], x_send.at[side, m])
+        for m, size in ((4, piece), (5, cuts[0]), (6, cuts[1])):
+            await_bytes(ot_v.at[pl.ds(0, size)], x_send.at[side, m])
     @pl.when(z != y)
     def _():
         await_bytes(nz_low.at[0], nz_send)
@@ -483,10 +515,10 @@
             pltpu.VMEM((8, half), F32),
             pltpu.VMEM((2 * RING, 8, 128), F32),
             pltpu.VMEM((7, 8, 128), F32),
-            dma((3,)), dma((2, 6)), dma((2, 6)),
+            dma((3,)), dma((2, 7)), dma((2, 7)),
             dma((2, RING)), dma((2, RING)), dma((2, RING)), dma((2, RING)), dma((2, RING)),
             dma((2,)), dma((2,)), dma((2,)), dma((2,)),
-            dma, dma, dma, dma, dma, dma, dma, dma,
+            dma, dma, dma, dma, dma, dma, dma, dma, dma,
             dma((2,)), dma((2, 3)), dma((2, RING)), dma((2, RING, 3)),
         ],
         compiler_params=pltpu.CompilerParams(

time: 141 us -> 140 us (level)
  no operation moved by 1% of the time
where the time goes in v5:
time: 140 us; the launch traced here: 139 us
  Pallas kernels  135 us (96%)
  local copies, waits for them, and re-layouts  4.13 us (3%)
    pallas_call x1, Pallas kernels, on_device(): pl.pallas_call(functools.partial(kernel, bound), out_shape=pltpu.VMEM((wi...  135 us
    unnamed x1, local copies, waits for them, and re-layouts  4.13 us

profile of v5, /device:TPU:0, one launch (start us, length us, event | category | flops | bytes accessed | tf_op | source)
XLA Modules:
  0.0 139.5 jit_solution(4059083308015066304)
XLA Ops:
  0.7 134.7 %shard_map.46 = bf16[2304,2304]{1,0:T(8,128)(2,1)S(1)} custom-call(s32[1]{0:T(128)S(6)} %copy.7.len_ref, bf16[576,1024]{1,0:T(8,128)(2,1)} %bitcast.9, bf16[1024,2304]{1,0:T(8,128)(2,1)} %bitcast.7, f32[144,2304]{1,0:T(8,128)} %bitcast.8), custom_call_target="tpu_custom_call" | custom-call | flops 10871635968 | bytes 30000000 | tf_op jit(solution)/shard_map/pallas_call | solution.py:496
  135.3 4.1 %copy.6 = bf16[1,2304,2304]{2,1,0:T(8,128)(2,1)} copy(bf16[1,2304,2304]{2,1,0:T(8,128)(2,1)S(1)} %bitcast.6) | data formatting | bytes 21233664

commit v6 on v5

--- a/solution.py
+++ b/solution.py
@@ -60,6 +60,10 @@
         other = (me + k) % (2 * RING)
         group.append({"tensor": other // 2, "layer": other % 2})
 
+    barrier = pltpu.get_barrier_semaphore()
+    for device in group + [z_up, z_down, z_far, y_up, y_down, y_far]:
+        pl.semaphore_signal(barrier, inc=1, device_id=device, device_id_type=MESH)
+
     own = pl.multiple_of(x * block, 16)
     load_o = pltpu.make_async_copy(o_hbm, ot_v.at[pl.ds(own, block)], load_sem.at[1])
     load_o.start()
@@ -67,10 +71,6 @@
     load_h.start()
     load_n = pltpu.make_async_copy(noise_hbm, nz, load_sem.at[2])
     load_n.start()
-
-    barrier = pltpu.get_barrier_semaphore()
-    for device in group + [z_up, z_down, z_far, y_up, y_down, y_far]:
-        pl.semaphore_signal(barrier, inc=1, device_id=device, device_id_type=MESH)
 
     def passed_on(m):
         return m >= RING

time: 140 us -> 140 us (level)
  no operation moved by 1% of the time
where the time goes in v6:
time: 140 us; the launch traced here: 139 us
  Pallas kernels  135 us (96%)
  local copies, waits for them, and re-layouts  4.13 us (3%)
    pallas_call x1, Pallas kernels, on_device(): pl.pallas_call(functools.partial(kernel, bound), out_shape=pltpu.VMEM((wi...  135 us
    unnamed x1, local copies, waits for them, and re-layouts  4.13 us

profile of v6, /device:TPU:0, one launch (start us, length us, event | category | flops | bytes accessed | tf_op | source)
XLA Modules:
  0.0 139.5 jit_solution(13576972433744705285)
XLA Ops:
  0.7 134.7 %shard_map.46 = bf16[2304,2304]{1,0:T(8,128)(2,1)S(1)} custom-call(s32[1]{0:T(128)S(6)} %copy.7.len_ref, bf16[576,1024]{1,0:T(8,128)(2,1)} %bitcast.9, bf16[1024,2304]{1,0:T(8,128)(2,1)} %bitcast.7, f32[144,2304]{1,0:T(8,128)} %bitcast.8), custom_call_target="tpu_custom_call" | custom-call | flops 10871635968 | bytes 30000000 | tf_op jit(solution)/shard_map/pallas_call | solution.py:496
  135.3 4.1 %copy.6 = bf16[1,2304,2304]{2,1,0:T(8,128)(2,1)} copy(bf16[1,2304,2304]{2,1,0:T(8,128)(2,1)S(1)} %bitcast.6) | data formatting | bytes 21233664
